TPU v7x, 512 devices: a whole 4x4x16 slice. The times are simulated.
512 devices in a mesh: mp: 16 (over y, z_hi, core), row: 8 (over z_lo), col: 4 (over x).
Axes of the slice: x: 4, y: 4, z: 16 (z_hi: 2, z_lo: 8; z = z_hi * 8 + z_lo), core: 2. Of those that a mesh axis runs over, the one named last changes fastest.
Arguments:
- activations: bfloat16 [16, 512, 4096], P('mp', None, 'row'), as said below
- weights: bfloat16 [16, 4096, 2048], P('mp', None, ('row', 'col')), may hold values from -6 to 6
Outputs:
- merged: float32 [4096, 2048], P(('row', 'col'), 'mp')
Inputs may be any that keep to these rules, and one draw needn't show every extreme that they name: `activations`: calibration inputs of each checkpoint, features of differing scales.
All inputs are finite; a program needn't handle non-finite values.
Results may differ from a plain program's by a relative error of at most 0.0028.
Values may be sent and summed in bfloat16 or wider, within the bound.
A program may use at most 64 MiB of HBM per device.

v0:
```python
import jax
import jax.numpy as jnp
from jax import lax
from jax.sharding import PartitionSpec as P

ITERS = 3


def apply_gram(gram, vector):
    gathered = lax.all_gather(vector, "row", axis=0, tiled=True)
    partial_image = jnp.dot(
        gram, gathered, precision=lax.Precision.HIGHEST, preferred_element_type=jnp.float32
    )
    return lax.psum_scatter(partial_image, "col", scatter_dimension=0, tiled=True)


def column_norms(residual):
    return lax.psum(jnp.sum(residual * residual, axis=0), ("row", "col"))


def local(activations, weights):
    local_rows = activations[0]
    local_weight = weights[0]
    n_row = lax.axis_size("row")
    n_col = lax.axis_size("col")
    col_index = lax.axis_index("col")
    tokens = local_rows.shape[0]
    block = local_rows.shape[1] // n_col
    every_feature = lax.all_gather(local_rows, "row", axis=1, tiled=True)
    projected = jnp.dot(every_feature, local_weight, preferred_element_type=jnp.float32).astype(
        jnp.bfloat16
    )
    outputs = lax.all_gather(projected, ("row", "col"), axis=1, tiled=True)
    blocked = every_feature.reshape(tokens, n_row, n_col, block)
    picked = lax.dynamic_slice_in_dim(blocked, col_index, 1, 2).reshape(tokens, n_row * block)
    dims = (((0,), (0,)), ((), ()))
    gram_term = lax.dot_general(local_rows, picked, dims, preferred_element_type=jnp.float32)
    own_block = lax.dynamic_slice_in_dim(local_rows, col_index * block, block, 1)
    rhs_term = lax.dot_general(own_block, outputs, dims, preferred_element_type=jnp.float32)
    gram = lax.psum(gram_term, "mp")
    rhs = lax.psum_scatter(rhs_term, "mp", scatter_dimension=1, tiled=True)
    merged = jnp.zeros_like(rhs)
    residual = rhs
    direction = rhs
    norm_now = column_norms(residual)
    for step in range(ITERS):
        image = apply_gram(gram, direction)
        curvature = lax.psum(jnp.sum(direction * image, axis=0), ("row", "col"))
        alpha = norm_now / curvature
        merged = merged + alpha * direction
        residual = residual - alpha * image
        norm_next = column_norms(residual)
        direction = residual + norm_next / norm_now * direction
        norm_now = norm_next
    return merged


def solution(mesh):
    in_specs = (P("mp", None, "row"), P("mp", None, ("row", "col")))
    out_specs = P(("row", "col"), "mp")
    return jax.shard_map(local, mesh=mesh, in_specs=in_specs, out_specs=out_specs, check_vma=False)
```

profile of v0, /device:TPU:17, one launch (start us, length us, event | category | flops | bytes accessed | tf_op | source)
XLA Modules:
  0.0 1525.2 jit_solution(17468980028079951588)
XLA Ops:
  6.5 2.1 copy.3
  8.7 109.3 %all-gather.6.cloned.1.call-done = bf16[1,512,4096]{1,2,0:T(8,128)(2,1)} async-done(((bf16[1,512,512]{1,2,0:T(8,128)(2,1)}), bf16[1,512,4096]{1,2,0:T(8,128)(2,1)}) %all-gather.6.cloned.1.call-update) | async-done | bytes 4194320 | tf_op jit(solution)/shard_map/all_gather | solution.py:29
  118.0 3.7 fusion.2
  121.8 197.7 %all-gather.4.cloned.1.call-done = bf16[512,2048]{0,1:T(8,128)(2,1)} async-done(((bf16[512,64]{0,1:T(8,128)(2,1)}), bf16[512,2048]{0,1:T(8,128)(2,1)}) %all-gather.4.cloned.1.call-update) | async-done | bytes 2097168 | tf_op jit(solution)/shard_map/all_gather | solution.py:33
  319.4 3.4 fusion.7
  322.9 1.3 constant_dynamic-slice_fusion
  324.3 2.0 convolution_bitcast_fusion
  326.4 121.5 %reduce-scatter.5.cloned.1.call-done = f32[128,128]{1,0:T(8,128)} async-done(((f32[128,2048]{1,0:T(8,128)}), f32[128,128]{1,0:T(8,128)}) %reduce-scatter.5.cloned.1.call-update) | async-done | bytes 65552 | tf_op jit(solution)/shard_map/reduce_scatter | solution.py:41
  447.9 48.6 %all_gather.17 = f32[1024,128]{1,0:T(8,128)S(1)} all-gather(f32[128,128]{1,0:T(8,128)} %reduce-scatter.5.cloned.1.call-done), channel_id=1, replica_groups=mesh['mp'=16,'row'=8,'col'=4] {'row'}, dimensions={0}, use_global_device_ids=true | all-gather | bytes 589824 | tf_op jit(solution)/shard_map/all_gather | solution.py:10
  496.5 253.8 %all-reduce.3.cloned.1.call-done = f32[512,1024]{0,1:T(8,128)} async-done(((f32[512,1024]{0,1:T(8,128)}), f32[512,1024]{0,1:T(8,128)}) %all-reduce.3.cloned.1.call-update) | async-done | bytes 2097168 | tf_op jit(solution)/shard_map/psum | solution.py:40
  750.2 5.9 fusion.11
  756.2 32.9 %reduce-scatter.7.cloned.1.call-done = f32[128,128]{1,0:T(8,128)} async-done(((f32[512,128]{1,0:T(8,128)}), f32[128,128]{1,0:T(8,128)}) %reduce-scatter.7.cloned.1.call-update) | async-done | bytes 65552 | tf_op jit(solution)/shard_map/reduce_scatter | solution.py:14
  790.0 108.0 %all-reduce = (f32[128]{0:T(128)S(1)}, f32[128]{0:T(128)S(1)}) all-reduce(f32[128]{0:T(128)S(1)} %get-tuple-element.6, f32[128]{0:T(128)S(1)} %get-tuple-element.5), channel_id=1, replica_groups=mesh['mp'=16,'row'=8,'col'=4] {'row','col'}, use_global_device_ids=true, to_apply=%region_2.0 | all-reduce | flops 256 | bytes 2048 | tf_op jit(solution)/shard_map/psum | solution.py:18
  898.0 0.9 multiply_reduce_fusion.3
  898.9 98.9 %psum.52 = f32[128]{0:T(128)S(1)} all-reduce(f32[128]{0:T(128)S(1)} %get-tuple-element.9), channel_id=1, replica_groups=mesh['mp'=16,'row'=8,'col'=4] {'row','col'}, use_global_device_ids=true, to_apply=%region_8.0 | all-reduce | flops 128 | bytes 1024 | tf_op jit(solution)/shard_map/psum | solution.py:18
  997.8 41.5 %all_gather.18 = f32[1024,128]{1,0:T(8,128)S(1)} all-gather(f32[128,128]{1,0:T(8,128)S(1)} %multiply_add_fusion.2), channel_id=1, replica_groups=mesh['mp'=16,'row'=8,'col'=4] {'row'}, dimensions={0}, use_global_device_ids=true | all-gather | bytes 589824 | tf_op jit(solution)/shard_map/all_gather | solution.py:10
  1039.3 4.1 fusion.12
  1043.5 55.0 %reduce-scatter.9.cloned.1.call-done = f32[128,128]{1,0:T(8,128)} async-done(((f32[512,128]{1,0:T(8,128)}), f32[128,128]{1,0:T(8,128)}) %reduce-scatter.9.cloned.1.call-update) | async-done | bytes 65552 | tf_op jit(solution)/shard_map/reduce_scatter | solution.py:14
  1099.3 108.0 %psum.53 = f32[128]{0:T(128)S(1)} all-reduce(f32[128]{0:T(128)S(1)} %multiply_reduce_fusion.2), channel_id=1, replica_groups=mesh['mp'=16,'row'=8,'col'=4] {'row','col'}, use_global_device_ids=true, to_apply=%region_11.0 | all-reduce | flops 128 | bytes 1024 | tf_op jit(solution)/shard_map/psum | solution.py:48
  1208.2 98.9 %psum.54 = f32[128]{0:T(128)S(1)} all-reduce(f32[128]{0:T(128)S(1)} %multiply_reduce_fusion.1), channel_id=1, replica_groups=mesh['mp'=16,'row'=8,'col'=4] {'row','col'}, use_global_device_ids=true, to_apply=%region_13.0 | all-reduce | flops 128 | bytes 1024 | tf_op jit(solution)/shard_map/psum | solution.py:18
  1307.9 41.5 %all_gather.19 = f32[1024,128]{1,0:T(8,128)S(1)} all-gather(f32[128,128]{1,0:T(8,128)S(1)} %multiply_add_fusion.1), channel_id=1, replica_groups=mesh['mp'=16,'row'=8,'col'=4] {'row'}, dimensions={0}, use_global_device_ids=true | all-gather | bytes 589824 | tf_op jit(solution)/shard_map/all_gather | solution.py:10
  1349.5 4.1 fusion.13
  1353.6 55.2 %reduce-scatter.11.cloned.1.call-done = f32[128,128]{1,0:T(8,128)} async-done(((f32[512,128]{1,0:T(8,128)}), f32[128,128]{1,0:T(8,128)}) %reduce-scatter.11.cloned.1.call-update) | async-done | bytes 65552 | tf_op jit(solution)/shard_map/reduce_scatter | solution.py:14
  1409.6 108.0 %psum.55 = f32[128]{0:T(128)S(1)} all-reduce(f32[128]{0:T(128)S(1)} %multiply_reduce_fusion), channel_id=1, replica_groups=mesh['mp'=16,'row'=8,'col'=4] {'row','col'}, use_global_device_ids=true, to_apply=%region_16.0 | all-reduce | flops 128 | bytes 1024 | tf_op jit(solution)/shard_map/psum | solution.py:48
  (34 shorter events, 5.4 us)
Async XLA Ops:
  6.5 111.5 %copy-start = (bf16[1,4096,64]{1,2,0:T(8,128)(2,1)S(1)}, bf16[1,4096,64]{1,2,0:T(8,128)(2,1)}, u32[]{:S(2)}) copy-start(bf16[1,4096,64]{1,2,0:T(8,128)(2,1)} %param.3) | copy-start | bytes 1572868
  6.5 111.5 %all-gather.6.cloned.1.call-start = ((), (), s32[]{:S(2)}) async-start(), calls=%async_computation.10 | async-start | bytes 4718592 | tf_op jit(solution)/shard_map/all_gather | solution.py:29
  8.7 310.8 %copy-start.2 = (bf16[1,512,512]{2,1,0:T(8,128)(2,1)S(1)}, bf16[1,512,512]{2,1,0:T(8,128)(2,1)}, u32[]{:S(2)}) copy-start(bf16[1,512,512]{2,1,0:T(8,128)(2,1)} %param.2) | copy-start | bytes 1572868
  8.7 310.8 %all-gather.4.cloned.1.call-start = ((), (), s32[]{:S(2)}) async-start(), calls=%async_computation.4 | async-start | bytes 2162688 | tf_op jit(solution)/shard_map/all_gather | solution.py:33
  121.7 326.1 %reduce-scatter.5.cloned.1.call-start = ((), (), s32[]{:S(2)}) async-start(), calls=%async_computation.5 | async-start | bytes 1114112 | tf_op jit(solution)/shard_map/reduce_scatter | solution.py:41
  322.9 427.4 %all-reduce.3.cloned.1.call-start = ((), (), s32[]{:S(2)}) async-start(), calls=%async_computation.6 | async-start | bytes 4194304 | tf_op jit(solution)/shard_map/psum | solution.py:40
  326.3 462.8 %reduce-scatter.7.cloned.1.call-start = ((), (), s32[]{:S(2)}) async-start(), calls=%async_computation.7 | async-start | bytes 327680 | tf_op jit(solution)/shard_map/reduce_scatter | solution.py:14
  447.9 341.2 %copy-start.3 = (f32[128,128]{1,0:T(8,128)S(1)}, f32[128,128]{1,0:T(8,128)}, u32[]{:S(2)}) copy-start(f32[128,128]{1,0:T(8,128)} %reduce-scatter.5.cloned.1.call-done) | copy-start | bytes 196612
  750.2 289.1 %copy-start.1 = (f32[512,1024]{0,1:T(8,128)S(1)}, f32[512,1024]{0,1:T(8,128)}, u32[]{:S(2)}) copy-start(f32[512,1024]{0,1:T(8,128)} %all-reduce.3.cloned.1.call-done) | copy-start | bytes 6291460
  756.2 342.3 %reduce-scatter.9.cloned.1.call-start = ((), (), s32[]{:S(2)}) async-start(), calls=%async_computation.8 | async-start | bytes 327680 | tf_op jit(solution)/shard_map/reduce_scatter | solution.py:14
  1043.4 365.3 %reduce-scatter.11.cloned.1.call-start = ((), (), s32[]{:S(2)}) async-start(), calls=%async_computation.9 | async-start | bytes 327680 | tf_op jit(solution)/shard_map/reduce_scatter | solution.py:14
Sparse Core Ops, SparseCore 0:
  9.4 108.5 all-gather.5
  121.8 197.5 all-gather.3
  324.1 123.6 reduce-scatter.4
  450.9 299.2 all-reduce.2
  756.3 32.7 reduce-scatter.6
  1043.6 54.8 reduce-scatter.8
  1353.7 55.0 reduce-scatter.10
where the time goes:
time: 1540 us; the launch traced here: 1530 us
  waiting for transfers between devices  825 us (54%)
  blocking collectives  653 us (42%)
  matrix products  23.2 us (2%)
    psum x3, blocking collectives, column_norms(): return lax.psum(jnp.sum(residual * residual, axis=0), ('row', 'col'))  306 us
    psum x1, waiting for transfers between devices, local(): gram = lax.psum(gram_term, 'mp')  254 us
    psum x2, blocking collectives, local(): curvature = lax.psum(jnp.sum(direction * image, axis=0), ('row', 'col'))  216 us
    all_gather x1, waiting for transfers between devices, local(): outputs = lax.all_gather(projected, ('row', 'col'), axis=1, tiled=True)  198 us
    reduce_scatter x3, waiting for transfers between devices, apply_gram(): lax.psum_scatter(partial_image, 'col', scatter_dimension=0, tiled=True)  143 us
    all_gather x3, blocking collectives, apply_gram(): gathered = lax.all_gather(vector, 'row', axis=0, tiled=True)  132 us
    reduce_scatter x1, waiting for transfers between devices, local(): rhs = lax.psum_scatter(rhs_term, 'mp', scatter_dimension=1, tiled=True)  122 us
    all_gather x1, waiting for transfers between devices, local(): every_feature = lax.all_gather(local_rows, 'row', axis=1, tiled=True)  109 us
  transfers between devices with their start and end apart: 7, of which 7 were waited for; matrix products, arithmetic and copies ran while one was open for 0% of the time, Pallas kernels for 0%

commit v1 on v0

v1 whole, which is shorter than its diff:
```python
import jax
import jax.numpy as jnp
from jax import lax
from jax.experimental import pallas as pl
from jax.experimental.pallas import tpu as pltpu
from jax.sharding import PartitionSpec as P

MESH = pl.DeviceIdType.MESH
F32 = jnp.float32
BF16 = jnp.bfloat16
NZ = 192
SH = 80
H0 = 48
COLS = 32


def fold(v):
    return v[:, :128] + v[:, 128:256] + v[:, 256:384] + v[:, 384:]


def kernel(
    a_hbm, w_hbm, out_ref,
    abuf, wbuf, yown, ycat, thl, ubuf, rbuf, img, res, dir1, dir2, dhl, curv, mblk, obuf,
    in_sem, zs, zr, xs, xr, fs, fr, ys, yr, us, ur, gs, gr, cs, cr, os, orr,
):
    mp = lax.axis_index("mp")
    zl = lax.axis_index("row")
    x = lax.axis_index("col")
    y = lax.div(mp, 4)
    zh = lax.rem(lax.div(mp, 2), 2)
    k = lax.rem(mp, 2)
    z = 8 * zh + zl
    me = 2 * y + k

    def dev(dx, dy, dz, dk):
        return (4 * dy + 2 * lax.div(dz, 8) + dk, lax.rem(dz, 8), dx)

    def remote(src, dst, send, recv, device):
        return pltpu.make_async_remote_copy(
            src_ref=src, dst_ref=dst, send_sem=send, recv_sem=recv, device_id=device, device_id_type=MESH
        )

    def at_z(d):
        return lax.rem(z + d + 16, 16)

    def at_x(d):
        return lax.rem(x + d + 4, 4)

    def member(b):
        return (4 * lax.div(b, 2) + 2 * zh + lax.rem(b, 2), zl, x)

    in_a = pltpu.make_async_copy(a_hbm.at[0], abuf.at[z], in_sem.at[0])
    in_w = pltpu.make_async_copy(w_hbm.at[0], wbuf, in_sem.at[1])
    in_a.start()
    in_w.start()

    to_y, to_z, to_k = lax.div(zl, 2), 8 * lax.rem(zl, 2) + me, lax.div(x, 2)
    from_y, from_k = lax.div(zl, 2), lax.rem(zl, 2)

    def out_self(dx):
        return (dx == x) & (to_y == y) & (to_z == z) & (to_k == k)

    def source(i, h):
        return 2 * k + i, from_y, 8 * h + 2 * y + zh, from_k

    barrier = pltpu.get_barrier_semaphore()

    def greet(device):
        pl.semaphore_signal(barrier, inc=1, device_id=device, device_id_type=MESH)

    greet(dev(x, y, at_z(1), k))
    greet(dev(x, y, at_z(-1), k))
    greet(dev(x, y, at_z(8), k))
    greet(dev(at_x(1), y, z, k))
    greet(dev(at_x(-1), y, z, k))

    @pl.loop(1, 8)
    def _(j):
        greet(member(lax.rem(me + j, 8)))

    selfs = jnp.int32(0)
    for i in range(2):
        for h in range(2):
            sx, sy, sz, sk = source(i, h)
            mine = (sx == x) & (sy == y) & (sz == z) & (sk == k)
            selfs = selfs + mine.astype(jnp.int32)

            @pl.when(jnp.logical_not(mine))
            def _():
                greet(dev(sx, sy, sz, sk))

    in_a.wait()
    in_w.wait()
    pl.semaphore_wait(barrier, 16 - selfs)

    def rows_of(part, shard):
        if part == 0:
            return pl.ds(0, NZ)
        return pl.ds(pl.multiple_of(NZ + SH * shard, 16), SH)

    def zcopy(d, part, s):
        sign = 1 - 2 * d
        ref = abuf.at[at_z(-sign * s), rows_of(part, x)]
        return remote(ref, ref, zs.at[d, part, s], zr.at[d, part, s], dev(x, y, at_z(sign), k))

    def zrecv(d, part, s):
        sign = 1 - 2 * d
        ref = abuf.at[at_z(-sign * (s + 1)), rows_of(part, x)]
        return remote(ref, ref, zs.at[d, part, s], zr.at[d, part, s], dev(x, y, at_z(sign), k))

    def xcopy(d, b):
        ref = abuf.at[b, rows_of(1, x)]
        return remote(ref, ref, xs.at[d, b], xr.at[d, b], dev(at_x(1 - 2 * d), y, z, k))

    def xrecv(d, b):
        ref = abuf.at[b, rows_of(1, at_x(2 * d - 1))]
        return remote(ref, ref, xs.at[d, b], xr.at[d, b], dev(at_x(1 - 2 * d), y, z, k))

    def half_rows(d, shard):
        if d == 0:
            return pl.ds(pl.multiple_of(NZ + SH * shard, 16), H0)
        return pl.ds(pl.multiple_of(NZ + SH * shard + H0, 16), SH - H0)

    def fcopy(d, b):
        ref = abuf.at[b, half_rows(d, at_x(2 * d - 1))]
        return remote(ref, ref, fs.at[d, b], fr.at[d, b], dev(at_x(1 - 2 * d), y, z, k))

    def frecv(d, b):
        ref = abuf.at[b, half_rows(d, at_x(2))]
        return remote(ref, ref, fs.at[d, b], fr.at[d, b], dev(at_x(1 - 2 * d), y, z, k))

    def pass_on(b):
        for d in range(2):
            xrecv(d, b).wait_recv()
            fcopy(d, b).start()

    for part in (1, 0):
        for d in range(2):
            zcopy(d, part, 0).start()

    @pl.loop(1, 9)
    def _(s):
        @pl.when(s <= 7)
        def _():
            zrecv(0, 1, s - 1).wait_recv()

            @pl.when(s <= 6)
            def _():
                zcopy(0, 1, s).start()

            for d in range(2):
                xcopy(d, at_z(-s)).start()

        zrecv(1, 1, s - 1).wait_recv()

        @pl.when(s <= 7)
        def _():
            zcopy(1, 1, s).start()

        for d in range(2):
            xcopy(d, at_z(s)).start()

        zrecv(0, 0, s - 1).wait_recv()

        @pl.when(s <= 7)
        def _():
            zcopy(0, 0, s).start()
            zrecv(1, 0, s - 1).wait_recv()

            @pl.when(s <= 6)
            def _():
                zcopy(1, 0, s).start()

        @pl.when(s >= 2)
        def _():
            pass_on(at_z(1 - s))
            pass_on(at_z(s - 1))

    pass_on(at_z(8))

    @pl.loop(1, 16)
    def _(j):
        for d in range(2):
            frecv(d, at_z(j)).wait_recv()
            xcopy(d, at_z(j)).wait_send()
            fcopy(d, at_z(j)).wait_send()

    @pl.loop(0, 8)
    def _(s):
        zcopy(0, 0, s).wait_send()
        zcopy(1, 1, s).wait_send()

        @pl.when(s <= 6)
        def _():
            zcopy(0, 1, s).wait_send()
            zcopy(1, 0, s).wait_send()

    def project(b, acc):
        w = wbuf[pl.ds(pl.multiple_of(512 * b, 512), 512), :]
        return acc + lax.dot_general(
            w, abuf[8 * zh + b], (((0,), (1,)), ((), ())), preferred_element_type=F32
        )

    yown[...] = lax.fori_loop(0, 8, project, jnp.zeros((2 * COLS, 512), F32)).astype(BF16)
    away = yown.at[pl.ds(pl.multiple_of(COLS * (1 - zh), COLS), COLS)]
    ycopy = remote(away, ycat.at[zh], ys, yr, dev(x, y, at_z(8), k))
    ycopy.start()
    ycat[zh] = yown[pl.ds(pl.multiple_of(COLS * zh, COLS), COLS)]
    remote(away, ycat.at[1 - zh], ys, yr, dev(x, y, at_z(8), k)).wait_recv()
    ycopy.wait_send()

    def all_reduce(rnd, block):
        def part(b):
            return remote(ubuf.at[b], rbuf.at[rnd, me], us.at[rnd, b], ur.at[rnd, me], member(b))

        def part_from(b):
            return remote(ubuf.at[b], rbuf.at[rnd, b], us.at[rnd, b], ur.at[rnd, b], member(b))

        def whole(b):
            return remote(img.at[rnd, me], img.at[rnd, me], gs.at[rnd, b], gr.at[rnd, me], member(b))

        def whole_from(b):
            return remote(img.at[rnd, b], img.at[rnd, b], gs.at[rnd, b], gr.at[rnd, b], member(b))

        @pl.loop(1, 8)
        def _(j):
            b = lax.rem(me + j, 8)
            ubuf[b] = block(b)
            part(b).start()

        rbuf[rnd, me] = block(me)

        @pl.loop(1, 8)
        def _(j):
            part_from(lax.rem(me + j, 8)).wait_recv()

        total = rbuf[rnd, 0]
        for b in range(1, 8):
            total = total + rbuf[rnd, b]
        img[rnd, me] = total

        @pl.loop(1, 8)
        def _(j):
            whole(lax.rem(me + j, 8)).start()

        @pl.loop(1, 8)
        def _(j):
            b = lax.rem(me + j, 8)
            whole_from(b).wait_recv()
            whole(b).wait_send()
            part(b).wait_send()

    def split(v):
        hi = v.astype(BF16)
        return hi, (v - hi.astype(F32)).astype(BF16)

    def set_direction(b, v):
        hi, lo = split(v)
        dhl[b, pl.ds(0, COLS)] = hi
        dhl[b, pl.ds(COLS, COLS)] = lo

    def tokens_times(h):
        def step(b, acc):
            return acc + lax.dot_general(
                dhl[b], abuf[8 * h + b], (((1,), (1,)), ((), ())), preferred_element_type=F32
            )

        both = lax.fori_loop(0, 8, step, jnp.zeros((2 * COLS, 512), F32))
        return both[:COLS] + both[COLS:]

    def rhs_block(b):
        return jnp.dot(ycat[0], abuf[b], preferred_element_type=F32) + jnp.dot(
            ycat[1], abuf[8 + b], preferred_element_type=F32
        )

    def image_block(b):
        both = jnp.dot(thl[0], abuf[b], preferred_element_type=F32) + jnp.dot(
            thl[1], abuf[8 + b], preferred_element_type=F32
        )
        return both[:COLS] + both[COLS:]

    def apply_gram(rnd):
        for h in range(2):
            hi, lo = split(tokens_times(h))
            thl[h, pl.ds(0, COLS)] = hi
            thl[h, pl.ds(COLS, COLS)] = lo
        all_reduce(rnd, image_block)

    def column_sum(term):
        acc = jnp.zeros((COLS, 128), F32)
        for b in range(8):
            acc = acc + fold(term(b))
        return jnp.sum(acc, axis=1, keepdims=True)

    all_reduce(0, rhs_block)
    norm = column_sum(lambda b: img[0, b] * img[0, b])
    for b in range(8):
        set_direction(b, img[0, b])
    apply_gram(1)
    alpha0 = norm / column_sum(lambda b: img[0, b] * img[1, b])
    for b in range(8):
        res[b] = img[0, b] - alpha0 * img[1, b]
    norm1 = column_sum(lambda b: res[b] * res[b])
    beta = norm1 / norm
    for b in range(8):
        dir1[b] = res[b] + beta * img[0, b]
        set_direction(b, dir1[b])
    apply_gram(2)
    alpha1 = norm1 / column_sum(lambda b: dir1[b] * img[2, b])
    for b in range(8):
        res[b] = res[b] - alpha1 * img[2, b]
    norm2 = column_sum(lambda b: res[b] * res[b])
    beta = norm2 / norm1
    for b in range(8):
        dir2[b] = res[b] + beta * dir1[b]
        set_direction(b, dir2[b])
    curvature = jnp.zeros((COLS, 128), F32)
    for h in range(2):
        image = tokens_times(h)
        curvature = curvature + fold(image * image)
    curv[me] = curvature

    def ccopy(b):
        return remote(curv.at[me], curv.at[me], cs.at[b], cr.at[me], member(b))

    def crecv(b):
        return remote(curv.at[b], curv.at[b], cs.at[b], cr.at[b], member(b))

    @pl.loop(1, 8)
    def _(j):
        ccopy(lax.rem(me + j, 8)).start()

    @pl.loop(1, 8)
    def _(j):
        b = lax.rem(me + j, 8)
        crecv(b).wait_recv()
        ccopy(b).wait_send()

    total = curv[0]
    for b in range(1, 8):
        total = total + curv[b]
    alpha2 = norm2 / jnp.sum(total, axis=1, keepdims=True)
    merged = alpha0 * img[0, me] + alpha1 * dir1[me] + alpha2 * dir2[me]

    slot = 2 * lax.rem(x, 2) + zh
    for dx in range(4):
        mblk[dx] = merged[:, 128 * dx : 128 * (dx + 1)]

    def ocopy(dx):
        return remote(mblk.at[dx], obuf.at[slot], os.at[dx], orr.at[slot], dev(dx, to_y, to_z, to_k))

    for dx in range(4):

        @pl.when(jnp.logical_not(out_self(dx)))
        def _():
            ocopy(dx).start()

        @pl.when(out_self(dx))
        def _():
            obuf[slot] = mblk[dx]

    for i in range(2):
        for h in range(2):
            sx, sy, sz, sk = source(i, h)
            mine = (sx == x) & (sy == y) & (sz == z) & (sk == k)

            @pl.when(jnp.logical_not(mine))
            def _():
                q = 2 * i + h
                remote(mblk.at[0], obuf.at[q], os.at[0], orr.at[q], dev(sx, sy, sz, sk)).wait_recv()

    for dx in range(4):

        @pl.when(jnp.logical_not(out_self(dx)))
        def _():
            ocopy(dx).wait_send()

    for q in range(4):
        out_ref[:, COLS * q : COLS * (q + 1)] = obuf[q].T


def local(activations, weights):
    dma = pltpu.SemaphoreType.DMA
    vmem = pltpu.VMEM
    return pl.pallas_call(
        kernel,
        out_shape=jax.ShapeDtypeStruct((128, 128), F32),
        in_specs=[pl.BlockSpec(memory_space=pl.ANY)] * 2,
        out_specs=pl.BlockSpec(memory_space=pltpu.VMEM),
        scratch_shapes=[
            vmem((16, 512, 512), BF16),
            vmem((4096, 64), BF16),
            vmem((2 * COLS, 512), BF16),
            vmem((2, COLS, 512), BF16),
            vmem((2, 2 * COLS, 512), BF16),
            vmem((8, COLS, 512), F32),
            vmem((3, 8, COLS, 512), F32),
            vmem((3, 8, COLS, 512), F32),
            vmem((8, COLS, 512), F32),
            vmem((8, COLS, 512), F32),
            vmem((8, COLS, 512), F32),
            vmem((8, 2 * COLS, 512), BF16),
            vmem((8, COLS, 128), F32),
            vmem((4, COLS, 128), F32),
            vmem((4, COLS, 128), F32),
            dma((2,)),
            dma((2, 2, 8)),
            dma((2, 2, 8)),
            dma((2, 16)),
            dma((2, 16)),
            dma((2, 16)),
            dma((2, 16)),
            dma,
            dma,
            dma((3, 8)),
            dma((3, 8)),
            dma((3, 8)),
            dma((3, 8)),
            dma((8,)),
            dma((8,)),
            dma((4,)),
            dma((4,)),
        ],
        compiler_params=pltpu.CompilerParams(
            collective_id=0, has_side_effects=True, vmem_limit_bytes=48 * 1024 * 1024
        ),
    )(activations, weights)


def solution(mesh):
    in_specs = (P("mp", None, "row"), P("mp", None, ("row", "col")))
    out_specs = P(("row", "col"), "mp")
    return jax.shard_map(local, mesh=mesh, in_specs=in_specs, out_specs=out_specs, check_vma=False)
```

time: 1540 us -> 162 us (0.11)
  the two profiles are of different devices: /device:TPU:17 before, /device:TPU:1 now
where the time goes in v1:
time: 162 us
  Pallas kernels  160 us (99%)
  local copies, waits for them, and re-layouts  2.21 us (1%)
    pallas_call x1, Pallas kernels, local(): pl.pallas_call(kernel, out_shape=jax.ShapeDtypeStruct((128, 128), F32), i...  160 us

profile of v1, /device:TPU:1, one launch (start us, length us, event | category | flops | bytes accessed | tf_op | source)
XLA Modules:
  0.0 162.3 jit_solution(11221791543007806203)
XLA Ops:
  0.0 0.0 copy-start
  0.0 1.6 copy.3.w_hbm
  1.6 0.0 copy-done
  1.6 160.1 %shard_map.28 = f32[128,128]{1,0:T(8,128)S(1)} custom-call(bf16[1,512,512]{2,1,0:T(8,128)(2,1)S(1)} %copy-done, bf16[1,4096,64]{2,1,0:T(8,128)(2,1)S(1)} %copy.3.w_hbm), custom_call_target="tpu_custom_call" | custom-call | tf_op jit(solution)/shard_map/pallas_call | solution.py:385
  161.7 0.6 copy.5
Async XLA Ops:
  0.0 1.6 copy-start

commit v2 on v1

v2 whole, which is shorter than its diff:
```python
import jax
import jax.numpy as jnp
from jax import lax
from jax.experimental import pallas as pl
from jax.experimental.pallas import tpu as pltpu
from jax.sharding import PartitionSpec as P

MESH = pl.DeviceIdType.MESH
F32 = jnp.float32
BF16 = jnp.bfloat16
NZ = 96
SH = 80
COLS = 32


def fold(v):
    return v[:, :128] + v[:, 128:256] + v[:, 256:384] + v[:, 384:]


def total_of(v):
    return jnp.sum(v, axis=1, keepdims=True)


def kernel(
    a_hbm, w_hbm, out_ref,
    abuf, wbuf, yacc, yown, ycat, thl, ubuf, cbuf, rbuf, img, res, dir1, vacc, tok, curv, mblk, obuf,
    in_sem, zs, zr, xs, xr, fs, fr, ys, yr, cs, cr, us, ur, gs, gr, hs, hr, ks, kr, os, orr,
):
    mp = lax.axis_index("mp")
    zl = lax.axis_index("row")
    x = lax.axis_index("col")
    y = lax.div(mp, 4)
    zh = lax.rem(lax.div(mp, 2), 2)
    k = lax.rem(mp, 2)
    z = 8 * zh + zl
    me = 2 * y + k

    def dev(dx, dy, dz, dk):
        return (4 * dy + 2 * lax.div(dz, 8) + dk, lax.rem(dz, 8), dx)

    def remote(src, dst, send, recv, device):
        return pltpu.make_async_remote_copy(
            src_ref=src, dst_ref=dst, send_sem=send, recv_sem=recv, device_id=device, device_id_type=MESH
        )

    def at_z(d):
        return lax.rem(z + d + 16, 16)

    def at_x(d):
        return lax.rem(x + d + 4, 4)

    def at_y(d):
        return lax.rem(y + d, 4)

    def member(b):
        return (4 * lax.div(b, 2) + 2 * zh + lax.rem(b, 2), zl, x)

    in_a = pltpu.make_async_copy(a_hbm.at[0], abuf.at[z], in_sem.at[0])
    in_w = pltpu.make_async_copy(w_hbm.at[0], wbuf, in_sem.at[1])
    in_a.start()
    in_w.start()

    barrier = pltpu.get_barrier_semaphore()

    def greet(device):
        pl.semaphore_signal(barrier, inc=1, device_id=device, device_id_type=MESH)

    greet(dev(x, y, at_z(1), k))
    greet(dev(x, y, at_z(-1), k))
    greet(dev(at_x(1), y, z, k))
    greet(dev(at_x(-1), y, z, k))

    @pl.loop(1, 8)
    def _(j):
        greet(member(lax.rem(me + j, 8)))

    in_a.wait()
    pl.semaphore_wait(barrier, 11)

    def rows_of(part, shard):
        if part < 2:
            return pl.ds(NZ * part, NZ)
        return pl.ds(pl.multiple_of(2 * NZ + SH * shard, 16), SH)

    def steps(d, part):
        return 8 if (part < 2) == (d == 0) else 7

    def zlink(d, part, s, distance):
        sign = 1 - 2 * d
        ref = abuf.at[at_z(-sign * distance), rows_of(part, x)]
        return remote(ref, ref, zs.at[d, part, s], zr.at[d, part, s], dev(x, y, at_z(sign), k))

    def zcopy(d, part, s):
        return zlink(d, part, s, s)

    def zrecv(d, part, s):
        return zlink(d, part, s, s + 1)

    def xcopy(d, b):
        ref = abuf.at[b, rows_of(2, x)]
        return remote(ref, ref, xs.at[d, b], xr.at[d, b], dev(at_x(1 - 2 * d), y, z, k))

    def xrecv(d, b):
        ref = abuf.at[b, rows_of(2, at_x(2 * d - 1))]
        return remote(ref, ref, xs.at[d, b], xr.at[d, b], dev(at_x(1 - 2 * d), y, z, k))

    def fcopy(d, b):
        ref = abuf.at[b, rows_of(2, at_x(2 * d - 1)), pl.ds(256 * d, 256)]
        return remote(ref, ref, fs.at[d, b], fr.at[d, b], dev(at_x(1 - 2 * d), y, z, k))

    def frecv(d, b):
        ref = abuf.at[b, rows_of(2, at_x(2)), pl.ds(256 * d, 256)]
        return remote(ref, ref, fs.at[d, b], fr.at[d, b], dev(at_x(1 - 2 * d), y, z, k))

    def pass_on(b):
        for d in range(2):
            xrecv(d, b).wait_recv()
            fcopy(d, b).start()

    def project(b):
        w = wbuf[:, pl.ds(pl.multiple_of(512 * lax.rem(b, 8), 512), 512)]
        yacc[...] += lax.dot_general(w, abuf[b], (((1,), (1,)), ((), ())), preferred_element_type=F32)

    def settle(b):
        for d in range(2):
            frecv(d, b).wait_recv()

        @pl.when(lax.div(b, 8) == zh)
        def _():
            project(b)

    for part in (2, 0, 1):
        for d in range(2):
            zcopy(d, part, 0).start()
    in_w.wait()
    yacc[...] = jnp.zeros_like(yacc)
    project(z)

    @pl.loop(1, 9)
    def _(s):
        def forward(d, part):
            n = steps(d, part)

            def body():
                zrecv(d, part, s - 1).wait_recv()

                def go():
                    zcopy(d, part, s).start()

                pl.when(s <= n - 1)(go)
                if part == 2:
                    for e in range(2):
                        xcopy(e, at_z((2 * d - 1) * s)).start()

            if n == 8:
                body()
            else:
                pl.when(s <= 7)(body)

        for part in (2, 0, 1):
            for d in range(2):
                forward(d, part)

        @pl.when(s >= 2)
        def _():
            pass_on(at_z(1 - s))
            pass_on(at_z(s - 1))

        @pl.when(s >= 3)
        def _():
            settle(at_z(2 - s))
            settle(at_z(s - 2))

    pass_on(at_z(8))
    settle(at_z(-7))
    settle(at_z(7))
    yown[...] = yacc[...].astype(BF16)
    away = yown.at[pl.ds(pl.multiple_of(COLS * (1 - zh), COLS), COLS)]
    partner = dev(x, y, at_z(8), k)
    ycopy = remote(away, ycat.at[zh], ys, yr, partner)
    ycopy.start()
    ycat[zh] = yown[pl.ds(pl.multiple_of(COLS * zh, COLS), COLS)]

    @pl.loop(0, 8)
    def _(b):
        ubuf[b] = jnp.dot(ycat[zh], abuf[8 * zh + b], preferred_element_type=F32)

    settle(at_z(8))

    @pl.loop(1, 16)
    def _(j):
        for d in range(2):
            xcopy(d, at_z(j)).wait_send()
            fcopy(d, at_z(j)).wait_send()

    for d in range(2):
        for part in range(3):

            @pl.loop(0, steps(d, part))
            def _(s):
                zcopy(d, part, s).wait_send()

    remote(away, ycat.at[1 - zh], ys, yr, partner).wait_recv()
    ycopy.wait_send()

    sibling = dev(x, y, z, 1 - k)

    def all_reduce(rnd, block, arrive):
        def core_part(o):
            q = at_y(o)
            return remote(ubuf.at[2 * q + 1 - k], cbuf.at[rnd, q], cs.at[rnd, q], cr.at[rnd, q], sibling)

        def ring_part(o):
            q = at_y(o)
            return remote(ubuf.at[2 * q + k], rbuf.at[rnd, y], us.at[rnd, q], ur.at[rnd, y], dev(x, q, z, k))

        def ring_part_from(o):
            q = at_y(o)
            return remote(ubuf.at[2 * q + k], rbuf.at[rnd, q], us.at[rnd, q], ur.at[rnd, q], dev(x, q, z, k))

        def ring_whole(o):
            q = at_y(o)
            ref = img.at[rnd, me]
            return remote(ref, ref, gs.at[rnd, q], gr.at[rnd, y], dev(x, q, z, k))

        def ring_whole_from(o):
            q = at_y(o)
            ref = img.at[rnd, 2 * q + k]
            return remote(ref, ref, gs.at[rnd, q], gr.at[rnd, q], dev(x, q, z, k))

        def core_whole(o):
            q = at_y(o)
            ref = img.at[rnd, 2 * q + k]
            return remote(ref, ref, hs.at[rnd, q], hr.at[rnd, q], sibling)

        def core_whole_from(o):
            q = at_y(o)
            ref = img.at[rnd, 2 * q + 1 - k]
            return remote(ref, ref, hs.at[rnd, q], hr.at[rnd, q], sibling)

        def give(o):
            b = 2 * at_y(o) + 1 - k
            ubuf[b] = block(b)
            core_part(o).start()

        def keep(o):
            q = at_y(o)
            b = 2 * q + k
            mine = block(b)
            remote(ubuf.at[b], cbuf.at[rnd, q], cs.at[rnd, q], cr.at[rnd, q], sibling).wait_recv()
            if o:
                ubuf[b] = mine + cbuf[rnd, q]
                ring_part(o).start()
            else:
                img[rnd, me] = mine + cbuf[rnd, q]

        give(2)
        give(1)
        keep(2)
        give(3)
        keep(1)
        give(0)
        keep(3)
        keep(0)
        for o in (1, 3, 2):
            ring_part_from(o).wait_recv()
        img[rnd, me] += rbuf[rnd, at_y(1)] + rbuf[rnd, at_y(3)] + rbuf[rnd, at_y(2)]
        for o in (2, 1, 3):
            ring_whole(o).start()
        core_whole(0).start()
        arrive(me)
        core_whole_from(0).wait_recv()
        arrive(2 * y + 1 - k)
        for o in (1, 3, 2):
            ring_whole_from(o).wait_recv()
            core_whole(o).start()
            arrive(2 * at_y(o) + k)
        for o in (1, 3, 2):
            core_whole_from(o).wait_recv()
            arrive(2 * at_y(o) + 1 - k)
        for o in range(4):
            core_part(o).wait_send()
            core_whole(o).wait_send()
            if o:
                ring_part(o).wait_send()
                ring_whole(o).wait_send()

    def split(v):
        hi = v.astype(BF16)
        return hi, (v - hi.astype(F32)).astype(BF16)

    def tokens_times(v, b):
        both = jnp.concatenate(split(v), axis=0)
        for h in range(2):
            vacc[h] += lax.dot_general(
                both, abuf[8 * h + b], (((1,), (1,)), ((), ())), preferred_element_type=F32
            )

    def products(h):
        return vacc[h, :COLS] + vacc[h, COLS:]

    def set_tokens(h, v):
        hi, lo = split(v)
        thl[h, pl.ds(0, COLS)] = hi
        thl[h, pl.ds(COLS, COLS)] = lo

    def rhs_block(b):
        return ubuf[b] + jnp.dot(ycat[1 - zh], abuf[8 * (1 - zh) + b], preferred_element_type=F32)

    def image_block(b):
        both = jnp.dot(thl[0], abuf[b], preferred_element_type=F32) + jnp.dot(
            thl[1], abuf[8 + b], preferred_element_type=F32
        )
        return both[:COLS] + both[COLS:]

    def column_sum(term):
        acc = jnp.zeros((COLS, 128), F32)
        for b in range(8):
            acc = acc + fold(term(b))
        return total_of(acc)

    def arrived(rnd):
        def go(b):
            tokens_times(img[rnd, b], b)

        return go

    vacc[...] = jnp.zeros_like(vacc)
    all_reduce(0, rhs_block, arrived(0))
    for h in range(2):
        t = products(h)
        set_tokens(h, t)
        tok[0, h] = t
        tok[1, h] = t
    vacc[...] = jnp.zeros_like(vacc)
    all_reduce(1, image_block, arrived(1))
    norm = column_sum(lambda b: img[0, b] * img[0, b])
    alpha0 = norm / column_sum(lambda b: img[0, b] * img[1, b])
    for b in range(8):
        res[b] = img[0, b] - alpha0 * img[1, b]
    norm1 = column_sum(lambda b: res[b] * res[b])
    beta = norm1 / norm
    for h in range(2):
        t = tok[1, h] - alpha0 * products(h)
        tok[1, h] = t
        t = t + beta * tok[0, h]
        tok[0, h] = t
        set_tokens(h, t)
    for b in range(8):
        dir1[b] = res[b] + beta * img[0, b]
    vacc[...] = jnp.zeros_like(vacc)
    all_reduce(2, image_block, arrived(2))
    alpha1 = norm1 / column_sum(lambda b: dir1[b] * img[2, b])
    for b in range(8):
        res[b] = res[b] - alpha1 * img[2, b]
    norm2 = column_sum(lambda b: res[b] * res[b])
    beta = norm2 / norm1
    square = jnp.zeros((COLS, 128), F32)
    for h in range(2):
        t = tok[1, h] - alpha1 * products(h) + beta * tok[0, h]
        square = square + fold(t * t)
    curv[me] = square

    def kcopy(b):
        return remote(curv.at[me], curv.at[me], ks.at[b], kr.at[me], member(b))

    def krecv(b):
        return remote(curv.at[b], curv.at[b], ks.at[b], kr.at[b], member(b))

    @pl.loop(1, 8)
    def _(j):
        kcopy(lax.rem(me + j, 8)).start()

    known = alpha0 * img[0, me] + alpha1 * dir1[me]
    last = res[me] + beta * dir1[me]

    @pl.loop(1, 8)
    def _(j):
        b = lax.rem(me + j, 8)
        krecv(b).wait_recv()
        kcopy(b).wait_send()

    curvature = curv[0]
    for b in range(1, 8):
        curvature = curvature + curv[b]
    alpha2 = norm2 / total_of(curvature)
    merged = known + alpha2 * last

    to_y, to_z, to_k = lax.div(zl, 2), 8 * lax.rem(zl, 2) + me, lax.div(x, 2)
    from_y, from_k = lax.div(zl, 2), lax.rem(zl, 2)
    slot = 2 * lax.rem(x, 2) + zh

    def out_self(dx):
        return (dx == x) & (to_y == y) & (to_z == z) & (to_k == k)

    def ocopy(dx):
        return remote(mblk.at[dx], obuf.at[slot], os.at[dx], orr.at[slot], dev(dx, to_y, to_z, to_k))

    for dx in range(4):
        mblk[dx] = merged[:, 128 * dx : 128 * (dx + 1)]

        @pl.when(jnp.logical_not(out_self(dx)))
        def _():
            ocopy(dx).start()

        @pl.when(out_self(dx))
        def _():
            obuf[slot] = mblk[dx]

    for i in range(2):
        for h in range(2):
            q = 2 * i + h
            sx, sz = 2 * k + i, 8 * h + 2 * y + zh
            mine = (sx == x) & (from_y == y) & (sz == z) & (from_k == k)

            @pl.when(jnp.logical_not(mine))
            def _():
                remote(mblk.at[0], obuf.at[q], os.at[0], orr.at[q], dev(sx, from_y, sz, from_k)).wait_recv()

    for dx in range(4):

        @pl.when(jnp.logical_not(out_self(dx)))
        def _():
            ocopy(dx).wait_send()

    for q in range(4):
        out_ref[:, COLS * q : COLS * (q + 1)] = obuf[q].T


def local(activations, weights):
    dma = pltpu.SemaphoreType.DMA
    vmem = pltpu.VMEM
    return pl.pallas_call(
        kernel,
        out_shape=jax.ShapeDtypeStruct((128, 128), F32),
        in_specs=[pl.BlockSpec(memory_space=pl.ANY)] * 2,
        out_specs=pl.BlockSpec(memory_space=pltpu.VMEM),
        scratch_shapes=[
            vmem((16, 512, 512), BF16),
            vmem((2 * COLS, 4096), BF16),
            vmem((2 * COLS, 512), F32),
            vmem((2 * COLS, 512), BF16),
            vmem((2, COLS, 512), BF16),
            vmem((2, 2 * COLS, 512), BF16),
            vmem((8, COLS, 512), F32),
            vmem((3, 4, COLS, 512), F32),
            vmem((3, 4, COLS, 512), F32),
            vmem((3, 8, COLS, 512), F32),
            vmem((8, COLS, 512), F32),
            vmem((8, COLS, 512), F32),
            vmem((2, 2 * COLS, 512), F32),
            vmem((2, 2, COLS, 512), F32),
            vmem((8, COLS, 128), F32),
            vmem((4, COLS, 128), F32),
            vmem((4, COLS, 128), F32),
            dma((2,)),
            dma((2, 3, 8)),
            dma((2, 3, 8)),
            dma((2, 16)),
            dma((2, 16)),
            dma((2, 16)),
            dma((2, 16)),
            dma,
            dma,
            dma((3, 4)),
            dma((3, 4)),
            dma((3, 4)),
            dma((3, 4)),
            dma((3, 4)),
            dma((3, 4)),
            dma((3, 4)),
            dma((3, 4)),
            dma((8,)),
            dma((8,)),
            dma((4,)),
            dma((4,)),
        ],
        compiler_params=pltpu.CompilerParams(
            collective_id=0, has_side_effects=True, vmem_limit_bytes=62 * 1024 * 1024
        ),
    )(activations, jnp.swapaxes(weights, 1, 2))


def solution(mesh):
    in_specs = (P("mp", None, "row"), P("mp", None, ("row", "col")))
    out_specs = P(("row", "col"), "mp")
    return jax.shard_map(local, mesh=mesh, in_specs=in_specs, out_specs=out_specs, check_vma=False)
```

time: 162 us -> 135 us (0.83)
  Pallas kernels: 160 us -> 133 us
    pallas_call x1, Pallas kernels: 160 us -> 133 us  [local(): pl.pallas_call(kernel, out_shape=jax.ShapeDtypeStruct((128, 128), F32), i...]
where the time goes in v2:
time: 135 us
  Pallas kernels  133 us (99%)
  local copies, waits for them, and re-layouts  1.47 us (1%)
    pallas_call x1, Pallas kernels, local(): pl.pallas_call(kernel, out_shape=jax.ShapeDtypeStruct((128, 128), F32), i...  133 us

profile of v2, /device:TPU:1, one launch (start us, length us, event | category | flops | bytes accessed | tf_op | source)
XLA Modules:
  0.0 134.7 jit_solution(1516746639310655185)
XLA Ops:
  0.0 133.2 %shard_map.28 = f32[128,128]{1,0:T(8,128)} custom-call(bf16[1,512,512]{2,1,0:T(8,128)(2,1)} %a_hbm.1, bf16[1,64,4096]{2,1,0:T(8,128)(2,1)} %bitcast.1), custom_call_target="tpu_custom_call" | custom-call | tf_op jit(solution)/shard_map/pallas_call | solution.py:433
  133.2 1.5 %copy.4 = f32[128,128]{1,0:T(8,128)} copy(f32[128,128]{1,0:T(8,128)} %shard_map.28) | data formatting | bytes 131072

commit v3 on v2

--- a/solution.py
+++ b/solution.py
@@ -8,8 +8,10 @@
 MESH = pl.DeviceIdType.MESH
 F32 = jnp.float32
 BF16 = jnp.bfloat16
-NZ = 96
-SH = 80
+NZ = (96, 80)
+NP = len(NZ)
+ZS = sum(NZ)
+HALF = 176
 COLS = 32
 
 
@@ -23,8 +25,8 @@
 
 def kernel(
     a_hbm, w_hbm, out_ref,
-    abuf, wbuf, yacc, yown, ycat, thl, ubuf, cbuf, rbuf, img, res, dir1, vacc, tok, curv, mblk, obuf,
-    in_sem, zs, zr, xs, xr, fs, fr, ys, yr, cs, cr, us, ur, gs, gr, hs, hr, ks, kr, os, orr,
+    abuf, wbuf, yacc, yown, ycat, thl, ubuf, cbuf, rbuf, img, res, dir1, vacc, tok, dots, curv, mblk, obuf,
+    in_sem, zs, zr, xs, xr, fs, fr, es, er, ys, yr, cs, cr, us, ur, gs, gr, hs, hr, ks, kr, os, orr,
 ):
     mp = lax.axis_index("mp")
     zl = lax.axis_index("row")
@@ -77,17 +79,21 @@
     in_a.wait()
     pl.semaphore_wait(barrier, 11)
 
-    def rows_of(part, shard):
-        if part < 2:
-            return pl.ds(NZ * part, NZ)
-        return pl.ds(pl.multiple_of(2 * NZ + SH * shard, 16), SH)
+    def piece(b, part, shard):
+        if part < NP:
+            return abuf.at[b, pl.ds(sum(NZ[:part]), NZ[part])]
+        return abuf.at[b, pl.ds(ZS, 512 - ZS), pl.ds(pl.multiple_of(128 * shard, 128), 128)]
+
+    def half_piece(b, d, shard):
+        rows = pl.ds(ZS, HALF) if d == 0 else pl.ds(ZS + HALF, 512 - ZS - HALF)
+        return abuf.at[b, rows, pl.ds(pl.multiple_of(128 * shard, 128), 128)]
 
     def steps(d, part):
-        return 8 if (part < 2) == (d == 0) else 7
+        return 8 if (part < NP) == (d == 0) else 7
 
     def zlink(d, part, s, distance):
         sign = 1 - 2 * d
-        ref = abuf.at[at_z(-sign * distance), rows_of(part, x)]
+        ref = piece(at_z(-sign * distance), part, x)
         return remote(ref, ref, zs.at[d, part, s], zr.at[d, part, s], dev(x, y, at_z(sign), k))
 
     def zcopy(d, part, s):
@@ -97,20 +103,24 @@
         return zlink(d, part, s, s + 1)
 
     def xcopy(d, b):
-        ref = abuf.at[b, rows_of(2, x)]
+        ref = piece(b, NP, x)
         return remote(ref, ref, xs.at[d, b], xr.at[d, b], dev(at_x(1 - 2 * d), y, z, k))
 
     def xrecv(d, b):
-        ref = abuf.at[b, rows_of(2, at_x(2 * d - 1))]
+        ref = piece(b, NP, at_x(2 * d - 1))
         return remote(ref, ref, xs.at[d, b], xr.at[d, b], dev(at_x(1 - 2 * d), y, z, k))
 
     def fcopy(d, b):
-        ref = abuf.at[b, rows_of(2, at_x(2 * d - 1)), pl.ds(256 * d, 256)]
+        ref = half_piece(b, d, at_x(2 * d - 1))
         return remote(ref, ref, fs.at[d, b], fr.at[d, b], dev(at_x(1 - 2 * d), y, z, k))
 
     def frecv(d, b):
-        ref = abuf.at[b, rows_of(2, at_x(2)), pl.ds(256 * d, 256)]
+        ref = half_piece(b, d, at_x(2))
         return remote(ref, ref, fs.at[d, b], fr.at[d, b], dev(at_x(1 - 2 * d), y, z, k))
+
+    def finish(i, b):
+        ref = piece(b, NP, at_x((1, -1, 2)[i]))
+        return remote(ref, ref, es.at[i], er.at[i], dev(x, y, at_z(1 if i == 0 else -1), k))
 
     def pass_on(b):
         for d in range(2):
@@ -129,79 +139,92 @@
         def _():
             project(b)
 
-    for part in (2, 0, 1):
+    for part in (NP, *range(NP)):
         for d in range(2):
             zcopy(d, part, 0).start()
     in_w.wait()
     yacc[...] = jnp.zeros_like(yacc)
     project(z)
 
-    @pl.loop(1, 9)
+    @pl.loop(1, 8)
     def _(s):
-        def forward(d, part):
-            n = steps(d, part)
-
-            def body():
+        def forward(part):
+            for d in range(2):
                 zrecv(d, part, s - 1).wait_recv()
-
-                def go():
+                if steps(d, part) == 8:
                     zcopy(d, part, s).start()
-
-                pl.when(s <= n - 1)(go)
-                if part == 2:
+                else:
+
+                    @pl.when(s <= 6)
+                    def _():
+                        zcopy(d, part, s).start()
+
+                if part == NP:
                     for e in range(2):
                         xcopy(e, at_z((2 * d - 1) * s)).start()
 
-            if n == 8:
-                body()
-            else:
-                pl.when(s <= 7)(body)
-
-        for part in (2, 0, 1):
-            for d in range(2):
-                forward(d, part)
+        forward(NP)
 
         @pl.when(s >= 2)
         def _():
             pass_on(at_z(1 - s))
             pass_on(at_z(s - 1))
 
+        for part in range(NP):
+            forward(part)
+
         @pl.when(s >= 3)
         def _():
             settle(at_z(2 - s))
             settle(at_z(s - 2))
 
-    pass_on(at_z(8))
+    pass_on(at_z(7))
+    finish(1, at_z(7)).start()
+    pass_on(at_z(-7))
+    finish(0, at_z(-7)).start()
+    for d in (6, -6, 7):
+        settle(at_z(d))
+    finish(2, at_z(7)).start()
     settle(at_z(-7))
-    settle(at_z(7))
+
     yown[...] = yacc[...].astype(BF16)
-    away = yown.at[pl.ds(pl.multiple_of(COLS * (1 - zh), COLS), COLS)]
-    partner = dev(x, y, at_z(8), k)
-    ycopy = remote(away, ycat.at[zh], ys, yr, partner)
-    ycopy.start()
-    ycat[zh] = yown[pl.ds(pl.multiple_of(COLS * zh, COLS), COLS)]
-
-    @pl.loop(0, 8)
-    def _(b):
-        ubuf[b] = jnp.dot(ycat[zh], abuf[8 * zh + b], preferred_element_type=F32)
-
-    settle(at_z(8))
-
-    @pl.loop(1, 16)
+
+    def ycopy(i):
+        to = at_z(4 - 8 * i)
+        away = yown.at[pl.ds(pl.multiple_of(COLS * lax.div(to, 8), COLS), COLS)]
+        return remote(away, ycat.at[zh], ys.at[i], yr.at[i], dev(x, y, to, k))
+
+    def yrecv(i):
+        h = lax.div(at_z(8 * i - 4), 8)
+        return remote(yown.at[pl.ds(0, COLS)], ycat.at[h], ys.at[i], yr.at[i], dev(x, y, at_z(4 - 8 * i), k))
+
+    ycopy(0).start()
+    ycopy(1).start()
+
+    for part in range(NP):
+        zrecv(0, part, 7).wait_recv()
+    zrecv(1, NP, 7).wait_recv()
+    for i in range(3):
+        finish(i, at_z(8)).wait_recv()
+        finish(i, at_z(-7 if i == 0 else 7)).wait_send()
+
+    @pl.loop(1, 8)
     def _(j):
         for d in range(2):
-            xcopy(d, at_z(j)).wait_send()
-            fcopy(d, at_z(j)).wait_send()
+            for b in (at_z(j), at_z(-j)):
+                xcopy(d, b).wait_send()
+                fcopy(d, b).wait_send()
 
     for d in range(2):
-        for part in range(3):
+        for part in range(NP + 1):
 
             @pl.loop(0, steps(d, part))
             def _(s):
                 zcopy(d, part, s).wait_send()
 
-    remote(away, ycat.at[1 - zh], ys, yr, partner).wait_recv()
-    ycopy.wait_send()
+    for i in range(2):
+        yrecv(i).wait_recv()
+        ycopy(i).wait_send()
 
     sibling = dev(x, y, z, 1 - k)
 
@@ -305,7 +328,9 @@
         thl[h, pl.ds(COLS, COLS)] = lo
 
     def rhs_block(b):
-        return ubuf[b] + jnp.dot(ycat[1 - zh], abuf[8 * (1 - zh) + b], preferred_element_type=F32)
+        return jnp.dot(ycat[0], abuf[b], preferred_element_type=F32) + jnp.dot(
+            ycat[1], abuf[8 + b], preferred_element_type=F32
+        )
 
     def image_block(b):
         both = jnp.dot(thl[0], abuf[b], preferred_element_type=F32) + jnp.dot(
@@ -319,23 +344,27 @@
             acc = acc + fold(term(b))
         return total_of(acc)
 
-    def arrived(rnd):
+    def arrived(rnd, direction):
+        dots[...] = jnp.zeros_like(dots)
+
         def go(b):
-            tokens_times(img[rnd, b], b)
+            v = img[rnd, b]
+            tokens_times(v, b)
+            dots[...] += fold(v * direction(b))
 
         return go
 
     vacc[...] = jnp.zeros_like(vacc)
-    all_reduce(0, rhs_block, arrived(0))
+    all_reduce(0, rhs_block, arrived(0, lambda b: img[0, b]))
+    norm = total_of(dots[...])
     for h in range(2):
         t = products(h)
         set_tokens(h, t)
         tok[0, h] = t
         tok[1, h] = t
     vacc[...] = jnp.zeros_like(vacc)
-    all_reduce(1, image_block, arrived(1))
-    norm = column_sum(lambda b: img[0, b] * img[0, b])
-    alpha0 = norm / column_sum(lambda b: img[0, b] * img[1, b])
+    all_reduce(1, image_block, arrived(1, lambda b: img[0, b]))
+    alpha0 = norm / total_of(dots[...])
     for b in range(8):
         res[b] = img[0, b] - alpha0 * img[1, b]
     norm1 = column_sum(lambda b: res[b] * res[b])
@@ -349,8 +378,8 @@
     for b in range(8):
         dir1[b] = res[b] + beta * img[0, b]
     vacc[...] = jnp.zeros_like(vacc)
-    all_reduce(2, image_block, arrived(2))
-    alpha1 = norm1 / column_sum(lambda b: dir1[b] * img[2, b])
+    all_reduce(2, image_block, arrived(2, lambda b: dir1[b]))
+    alpha1 = norm1 / total_of(dots[...])
     for b in range(8):
         res[b] = res[b] - alpha1 * img[2, b]
     norm2 = column_sum(lambda b: res[b] * res[b])
@@ -359,7 +388,8 @@
     for h in range(2):
         t = tok[1, h] - alpha1 * products(h) + beta * tok[0, h]
         square = square + fold(t * t)
-    curv[me] = square
+    diagonal = lax.broadcasted_iota(jnp.int32, (COLS, 128), 0) == lax.broadcasted_iota(jnp.int32, (COLS, 128), 1)
+    curv[me] = jnp.sum(jnp.where(diagonal, total_of(square), 0.0), axis=0, keepdims=True)
 
     def kcopy(b):
         return remote(curv.at[me], curv.at[me], ks.at[b], kr.at[me], member(b))
@@ -383,10 +413,11 @@
     curvature = curv[0]
     for b in range(1, 8):
         curvature = curvature + curv[b]
-    alpha2 = norm2 / total_of(curvature)
+    alpha2 = norm2 / total_of(jnp.where(diagonal, curvature, 0.0))
     merged = known + alpha2 * last
 
-    to_y, to_z, to_k = lax.div(zl, 2), 8 * lax.rem(zl, 2) + me, lax.div(x, 2)
+    origin = lax.rem(zl + 4, 8)
+    to_y, to_z, to_k = lax.div(origin, 2), 8 * lax.rem(origin, 2) + me, lax.div(x, 2)
     from_y, from_k = lax.div(zl, 2), lax.rem(zl, 2)
     slot = 2 * lax.rem(x, 2) + zh
 
@@ -410,7 +441,7 @@
     for i in range(2):
         for h in range(2):
             q = 2 * i + h
-            sx, sz = 2 * k + i, 8 * h + 2 * y + zh
+            sx, sz = 2 * k + i, 8 * h + lax.rem(2 * y + zh + 4, 8)
             mine = (sx == x) & (from_y == y) & (sz == z) & (from_k == k)
 
             @pl.when(jnp.logical_not(mine))
@@ -450,18 +481,21 @@
             vmem((8, COLS, 512), F32),
             vmem((2, 2 * COLS, 512), F32),
             vmem((2, 2, COLS, 512), F32),
-            vmem((8, COLS, 128), F32),
+            vmem((COLS, 128), F32),
+            vmem((8, 1, 128), F32),
             vmem((4, COLS, 128), F32),
             vmem((4, COLS, 128), F32),
             dma((2,)),
-            dma((2, 3, 8)),
-            dma((2, 3, 8)),
+            dma((2, NP + 1, 8)),
+            dma((2, NP + 1, 8)),
             dma((2, 16)),
             dma((2, 16)),
             dma((2, 16)),
             dma((2, 16)),
-            dma,
-            dma,
+            dma((3,)),
+            dma((3,)),
+            dma((2,)),
+            dma((2,)),
             dma((3, 4)),
             dma((3, 4)),
             dma((3, 4)),
@@ -476,7 +510,7 @@
             dma((4,)),
         ],
         compiler_params=pltpu.CompilerParams(
-            collective_id=0, has_side_effects=True, vmem_limit_bytes=62 * 1024 * 1024
+            collective_id=0, has_side_effects=True, vmem_limit_bytes=53 * 1024 * 1024 + 512 * 1024
         ),
     )(activations, jnp.swapaxes(weights, 1, 2))
 

time: 135 us -> 128 us (0.948)
  the two profiles are of different devices: /device:TPU:1 before, /device:TPU:17 now
where the time goes in v3:
time: 128 us
  Pallas kernels  127 us (99%)
    pallas_call x1, Pallas kernels, local(): pl.pallas_call(kernel, out_shape=jax.ShapeDtypeStruct((128, 128), F32), i...  127 us

profile of v3, /device:TPU:17, one launch (start us, length us, event | category | flops | bytes accessed | tf_op | source)
XLA Modules:
  0.0 128.0 jit_solution(17141590409379842774)
XLA Ops:
  0.0 127.3 %shard_map.28 = f32[128,128]{1,0:T(8,128)S(1)} custom-call(bf16[1,512,512]{2,1,0:T(8,128)(2,1)} %a_hbm.1, bf16[1,64,4096]{2,1,0:T(8,128)(2,1)} %bitcast.1), custom_call_target="tpu_custom_call" | custom-call | tf_op jit(solution)/shard_map/pallas_call | solution.py:464
  127.4 0.6 copy.4

commit v4 on v3

--- a/solution.py
+++ b/solution.py
@@ -11,8 +11,8 @@
 NZ = (96, 80)
 NP = len(NZ)
 ZS = sum(NZ)
-HALF = 176
 COLS = 32
+CUTS = 2
 
 
 def fold(v):
@@ -26,7 +26,7 @@
 def kernel(
     a_hbm, w_hbm, out_ref,
     abuf, wbuf, yacc, yown, ycat, thl, ubuf, cbuf, rbuf, img, res, dir1, vacc, tok, dots, curv, mblk, obuf,
-    in_sem, zs, zr, xs, xr, fs, fr, es, er, ys, yr, cs, cr, us, ur, gs, gr, hs, hr, ks, kr, os, orr,
+    in_sem, zs, zr, xs, xr, es, er, ys, yr, cs, cr, us, ur, gs, gr, hs, hr, ks, kr, os, orr,
 ):
     mp = lax.axis_index("mp")
     zl = lax.axis_index("row")
@@ -71,23 +71,20 @@
     greet(dev(x, y, at_z(-1), k))
     greet(dev(at_x(1), y, z, k))
     greet(dev(at_x(-1), y, z, k))
+    greet(dev(at_x(2), y, z, k))
 
     @pl.loop(1, 8)
     def _(j):
         greet(member(lax.rem(me + j, 8)))
 
     in_a.wait()
-    pl.semaphore_wait(barrier, 11)
+    pl.semaphore_wait(barrier, 12)
 
     def piece(b, part, shard):
         if part < NP:
             return abuf.at[b, pl.ds(sum(NZ[:part]), NZ[part])]
         return abuf.at[b, pl.ds(ZS, 512 - ZS), pl.ds(pl.multiple_of(128 * shard, 128), 128)]
 
-    def half_piece(b, d, shard):
-        rows = pl.ds(ZS, HALF) if d == 0 else pl.ds(ZS + HALF, 512 - ZS - HALF)
-        return abuf.at[b, rows, pl.ds(pl.multiple_of(128 * shard, 128), 128)]
-
     def steps(d, part):
         return 8 if (part < NP) == (d == 0) else 7
 
@@ -102,42 +99,31 @@
     def zrecv(d, part, s):
         return zlink(d, part, s, s + 1)
 
-    def xcopy(d, b):
+    def xcopy(i, b):
         ref = piece(b, NP, x)
-        return remote(ref, ref, xs.at[d, b], xr.at[d, b], dev(at_x(1 - 2 * d), y, z, k))
-
-    def xrecv(d, b):
-        ref = piece(b, NP, at_x(2 * d - 1))
-        return remote(ref, ref, xs.at[d, b], xr.at[d, b], dev(at_x(1 - 2 * d), y, z, k))
-
-    def fcopy(d, b):
-        ref = half_piece(b, d, at_x(2 * d - 1))
-        return remote(ref, ref, fs.at[d, b], fr.at[d, b], dev(at_x(1 - 2 * d), y, z, k))
-
-    def frecv(d, b):
-        ref = half_piece(b, d, at_x(2))
-        return remote(ref, ref, fs.at[d, b], fr.at[d, b], dev(at_x(1 - 2 * d), y, z, k))
+        return remote(ref, ref, xs.at[i, b], xr.at[i, b], dev(at_x((1, -1, 2)[i]), y, z, k))
+
+    def xrecv(i, b):
+        ref = piece(b, NP, at_x((-1, 1, 2)[i]))
+        return remote(ref, ref, xs.at[i, b], xr.at[i, b], dev(at_x((1, -1, 2)[i]), y, z, k))
 
     def finish(i, b):
         ref = piece(b, NP, at_x((1, -1, 2)[i]))
         return remote(ref, ref, es.at[i], er.at[i], dev(x, y, at_z(1 if i == 0 else -1), k))
 
-    def pass_on(b):
-        for d in range(2):
-            xrecv(d, b).wait_recv()
-            fcopy(d, b).start()
-
     def project(b):
         w = wbuf[:, pl.ds(pl.multiple_of(512 * lax.rem(b, 8), 512), 512)]
         yacc[...] += lax.dot_general(w, abuf[b], (((1,), (1,)), ((), ())), preferred_element_type=F32)
 
-    def settle(b):
-        for d in range(2):
-            frecv(d, b).wait_recv()
-
+    def use(b):
         @pl.when(lax.div(b, 8) == zh)
         def _():
             project(b)
+
+    def settle(b):
+        for i in range(3):
+            xrecv(i, b).wait_recv()
+        use(b)
 
     for part in (NP, *range(NP)):
         for d in range(2):
@@ -160,15 +146,10 @@
                         zcopy(d, part, s).start()
 
                 if part == NP:
-                    for e in range(2):
-                        xcopy(e, at_z((2 * d - 1) * s)).start()
+                    for i in range(3):
+                        xcopy(i, at_z((2 * d - 1) * s)).start()
 
         forward(NP)
-
-        @pl.when(s >= 2)
-        def _():
-            pass_on(at_z(1 - s))
-            pass_on(at_z(s - 1))
 
         for part in range(NP):
             forward(part)
@@ -178,14 +159,19 @@
             settle(at_z(2 - s))
             settle(at_z(s - 2))
 
-    pass_on(at_z(7))
+    for d in (6, -6):
+        settle(at_z(d))
+    xrecv(0, at_z(7)).wait_recv()
     finish(1, at_z(7)).start()
-    pass_on(at_z(-7))
+    xrecv(1, at_z(-7)).wait_recv()
     finish(0, at_z(-7)).start()
-    for d in (6, -6, 7):
-        settle(at_z(d))
+    xrecv(2, at_z(7)).wait_recv()
     finish(2, at_z(7)).start()
-    settle(at_z(-7))
+    xrecv(1, at_z(7)).wait_recv()
+    use(at_z(7))
+    xrecv(0, at_z(-7)).wait_recv()
+    xrecv(2, at_z(-7)).wait_recv()
+    use(at_z(-7))
 
     yown[...] = yacc[...].astype(BF16)
 
@@ -210,10 +196,9 @@
 
     @pl.loop(1, 8)
     def _(j):
-        for d in range(2):
+        for i in range(3):
             for b in (at_z(j), at_z(-j)):
-                xcopy(d, b).wait_send()
-                fcopy(d, b).wait_send()
+                xcopy(i, b).wait_send()
 
     for d in range(2):
         for part in range(NP + 1):
@@ -233,23 +218,28 @@
             q = at_y(o)
             return remote(ubuf.at[2 * q + 1 - k], cbuf.at[rnd, q], cs.at[rnd, q], cr.at[rnd, q], sibling)
 
-        def ring_part(o):
-            q = at_y(o)
-            return remote(ubuf.at[2 * q + k], rbuf.at[rnd, y], us.at[rnd, q], ur.at[rnd, y], dev(x, q, z, k))
-
-        def ring_part_from(o):
-            q = at_y(o)
-            return remote(ubuf.at[2 * q + k], rbuf.at[rnd, q], us.at[rnd, q], ur.at[rnd, q], dev(x, q, z, k))
-
-        def ring_whole(o):
-            q = at_y(o)
-            ref = img.at[rnd, me]
-            return remote(ref, ref, gs.at[rnd, q], gr.at[rnd, y], dev(x, q, z, k))
-
-        def ring_whole_from(o):
-            q = at_y(o)
-            ref = img.at[rnd, 2 * q + k]
-            return remote(ref, ref, gs.at[rnd, q], gr.at[rnd, q], dev(x, q, z, k))
+        def cut(c):
+            return pl.ds(c * (COLS // CUTS), COLS // CUTS)
+
+        def ring_part(o, c):
+            q = at_y(o)
+            src, dst = ubuf.at[2 * q + k, cut(c)], rbuf.at[rnd, y, cut(c)]
+            return remote(src, dst, us.at[rnd, q, c], ur.at[rnd, y, c], dev(x, q, z, k))
+
+        def ring_part_from(o, c):
+            q = at_y(o)
+            src, dst = ubuf.at[2 * q + k, cut(c)], rbuf.at[rnd, q, cut(c)]
+            return remote(src, dst, us.at[rnd, q, c], ur.at[rnd, q, c], dev(x, q, z, k))
+
+        def ring_whole(o, c):
+            q = at_y(o)
+            ref = img.at[rnd, me, cut(c)]
+            return remote(ref, ref, gs.at[rnd, q, c], gr.at[rnd, y, c], dev(x, q, z, k))
+
+        def ring_whole_from(o, c):
+            q = at_y(o)
+            ref = img.at[rnd, 2 * q + k, cut(c)]
+            return remote(ref, ref, gs.at[rnd, q, c], gr.at[rnd, q, c], dev(x, q, z, k))
 
         def core_whole(o):
             q = at_y(o)
@@ -273,7 +263,7 @@
             remote(ubuf.at[b], cbuf.at[rnd, q], cs.at[rnd, q], cr.at[rnd, q], sibling).wait_recv()
             if o:
                 ubuf[b] = mine + cbuf[rnd, q]
-                ring_part(o).start()
+                ring_part(o, 0).start()
             else:
                 img[rnd, me] = mine + cbuf[rnd, q]
 
@@ -284,18 +274,25 @@
         keep(1)
         give(0)
         keep(3)
+        for c in range(1, CUTS):
+            for o in (2, 1, 3):
+                ring_part(o, c).start()
         keep(0)
-        for o in (1, 3, 2):
-            ring_part_from(o).wait_recv()
-        img[rnd, me] += rbuf[rnd, at_y(1)] + rbuf[rnd, at_y(3)] + rbuf[rnd, at_y(2)]
-        for o in (2, 1, 3):
-            ring_whole(o).start()
+        for c in range(CUTS):
+            for o in (1, 3, 2):
+                ring_part_from(o, c).wait_recv()
+            img[rnd, me, cut(c)] += (
+                rbuf[rnd, at_y(1), cut(c)] + rbuf[rnd, at_y(3), cut(c)] + rbuf[rnd, at_y(2), cut(c)]
+            )
+            for o in (2, 1, 3):
+                ring_whole(o, c).start()
         core_whole(0).start()
         arrive(me)
         core_whole_from(0).wait_recv()
         arrive(2 * y + 1 - k)
         for o in (1, 3, 2):
-            ring_whole_from(o).wait_recv()
+            for c in range(CUTS):
+                ring_whole_from(o, c).wait_recv()
             core_whole(o).start()
             arrive(2 * at_y(o) + k)
         for o in (1, 3, 2):
@@ -305,8 +302,9 @@
             core_part(o).wait_send()
             core_whole(o).wait_send()
             if o:
-                ring_part(o).wait_send()
-                ring_whole(o).wait_send()
+                for c in range(CUTS):
+                    ring_part(o, c).wait_send()
+                    ring_whole(o, c).wait_send()
 
     def split(v):
         hi = v.astype(BF16)
@@ -488,20 +486,18 @@
             dma((2,)),
             dma((2, NP + 1, 8)),
             dma((2, NP + 1, 8)),
-            dma((2, 16)),
-            dma((2, 16)),
-            dma((2, 16)),
-            dma((2, 16)),
+            dma((3, 16)),
+            dma((3, 16)),
             dma((3,)),
             dma((3,)),
             dma((2,)),
             dma((2,)),
             dma((3, 4)),
             dma((3, 4)),
-            dma((3, 4)),
-            dma((3, 4)),
-            dma((3, 4)),
-            dma((3, 4)),
+            dma((3, 4, CUTS)),
+            dma((3, 4, CUTS)),
+            dma((3, 4, CUTS)),
+            dma((3, 4, CUTS)),
             dma((3, 4)),
             dma((3, 4)),
             dma((8,)),

time: 128 us -> 136 us (1.062)
  Pallas kernels: 127 us -> 135 us
    pallas_call x1, Pallas kernels: 127 us -> 135 us  [local(): pl.pallas_call(kernel, out_shape=jax.ShapeDtypeStruct((128, 128), F32), i...]
where the time goes in v4:
time: 136 us
  Pallas kernels  135 us (99%)
    pallas_call x1, Pallas kernels, local(): pl.pallas_call(kernel, out_shape=jax.ShapeDtypeStruct((128, 128), F32), i...  135 us

profile of v4, /device:TPU:17, one launch (start us, length us, event | category | flops | bytes accessed | tf_op | source)
XLA Modules:
  0.0 135.9 jit_solution(1718977487209385451)
XLA Ops:
  0.0 135.2 %shard_map.28 = f32[128,128]{1,0:T(8,128)S(1)} custom-call(bf16[1,512,512]{2,1,0:T(8,128)(2,1)} %a_hbm.1, bf16[1,64,4096]{2,1,0:T(8,128)(2,1)} %bitcast.1), custom_call_target="tpu_custom_call" | custom-call | tf_op jit(solution)/shard_map/pallas_call | solution.py:462
  135.2 0.6 copy.4

commit v5 on v3

--- a/solution.py
+++ b/solution.py
@@ -13,6 +13,7 @@
 ZS = sum(NZ)
 HALF = 176
 COLS = 32
+CUTS = 2
 
 
 def fold(v):
@@ -233,23 +234,28 @@
             q = at_y(o)
             return remote(ubuf.at[2 * q + 1 - k], cbuf.at[rnd, q], cs.at[rnd, q], cr.at[rnd, q], sibling)
 
-        def ring_part(o):
-            q = at_y(o)
-            return remote(ubuf.at[2 * q + k], rbuf.at[rnd, y], us.at[rnd, q], ur.at[rnd, y], dev(x, q, z, k))
-
-        def ring_part_from(o):
-            q = at_y(o)
-            return remote(ubuf.at[2 * q + k], rbuf.at[rnd, q], us.at[rnd, q], ur.at[rnd, q], dev(x, q, z, k))
-
-        def ring_whole(o):
-            q = at_y(o)
-            ref = img.at[rnd, me]
-            return remote(ref, ref, gs.at[rnd, q], gr.at[rnd, y], dev(x, q, z, k))
-
-        def ring_whole_from(o):
-            q = at_y(o)
-            ref = img.at[rnd, 2 * q + k]
-            return remote(ref, ref, gs.at[rnd, q], gr.at[rnd, q], dev(x, q, z, k))
+        def cut(c):
+            return pl.ds(c * (COLS // CUTS), COLS // CUTS)
+
+        def ring_part(o, c):
+            q = at_y(o)
+            src, dst = ubuf.at[2 * q + k, cut(c)], rbuf.at[rnd, y, cut(c)]
+            return remote(src, dst, us.at[rnd, q, c], ur.at[rnd, y, c], dev(x, q, z, k))
+
+        def ring_part_from(o, c):
+            q = at_y(o)
+            src, dst = ubuf.at[2 * q + k, cut(c)], rbuf.at[rnd, q, cut(c)]
+            return remote(src, dst, us.at[rnd, q, c], ur.at[rnd, q, c], dev(x, q, z, k))
+
+        def ring_whole(o, c):
+            q = at_y(o)
+            ref = img.at[rnd, me, cut(c)]
+            return remote(ref, ref, gs.at[rnd, q, c], gr.at[rnd, y, c], dev(x, q, z, k))
+
+        def ring_whole_from(o, c):
+            q = at_y(o)
+            ref = img.at[rnd, 2 * q + k, cut(c)]
+            return remote(ref, ref, gs.at[rnd, q, c], gr.at[rnd, q, c], dev(x, q, z, k))
 
         def core_whole(o):
             q = at_y(o)
@@ -273,7 +279,7 @@
             remote(ubuf.at[b], cbuf.at[rnd, q], cs.at[rnd, q], cr.at[rnd, q], sibling).wait_recv()
             if o:
                 ubuf[b] = mine + cbuf[rnd, q]
-                ring_part(o).start()
+                ring_part(o, 0).start()
             else:
                 img[rnd, me] = mine + cbuf[rnd, q]
 
@@ -284,18 +290,25 @@
         keep(1)
         give(0)
         keep(3)
+        for c in range(1, CUTS):
+            for o in (2, 1, 3):
+                ring_part(o, c).start()
         keep(0)
-        for o in (1, 3, 2):
-            ring_part_from(o).wait_recv()
-        img[rnd, me] += rbuf[rnd, at_y(1)] + rbuf[rnd, at_y(3)] + rbuf[rnd, at_y(2)]
-        for o in (2, 1, 3):
-            ring_whole(o).start()
+        for c in range(CUTS):
+            for o in (1, 3, 2):
+                ring_part_from(o, c).wait_recv()
+            img[rnd, me, cut(c)] += (
+                rbuf[rnd, at_y(1), cut(c)] + rbuf[rnd, at_y(3), cut(c)] + rbuf[rnd, at_y(2), cut(c)]
+            )
+            for o in (2, 1, 3):
+                ring_whole(o, c).start()
         core_whole(0).start()
         arrive(me)
         core_whole_from(0).wait_recv()
         arrive(2 * y + 1 - k)
         for o in (1, 3, 2):
-            ring_whole_from(o).wait_recv()
+            for c in range(CUTS):
+                ring_whole_from(o, c).wait_recv()
             core_whole(o).start()
             arrive(2 * at_y(o) + k)
         for o in (1, 3, 2):
@@ -305,8 +318,9 @@
             core_part(o).wait_send()
             core_whole(o).wait_send()
             if o:
-                ring_part(o).wait_send()
-                ring_whole(o).wait_send()
+                for c in range(CUTS):
+                    ring_part(o, c).wait_send()
+                    ring_whole(o, c).wait_send()
 
     def split(v):
         hi = v.astype(BF16)
@@ -498,10 +512,10 @@
             dma((2,)),
             dma((3, 4)),
             dma((3, 4)),
-            dma((3, 4)),
-            dma((3, 4)),
-            dma((3, 4)),
-            dma((3, 4)),
+            dma((3, 4, CUTS)),
+            dma((3, 4, CUTS)),
+            dma((3, 4, CUTS)),
+            dma((3, 4, CUTS)),
             dma((3, 4)),
             dma((3, 4)),
             dma((8,)),

time: 128 us -> 126 us (0.984)
    pallas_call x1, Pallas kernels: 127 us -> 126 us  [local(): pl.pallas_call(kernel, out_shape=jax.ShapeDtypeStruct((128, 128), F32), i...]
where the time goes in v5:
time: 126 us
  Pallas kernels  126 us (100%)
    pallas_call x1, Pallas kernels, local(): pl.pallas_call(kernel, out_shape=jax.ShapeDtypeStruct((128, 128), F32), i...  126 us

profile of v5, /device:TPU:17, one launch (start us, length us, event | category | flops | bytes accessed | tf_op | source)
XLA Modules:
  0.0 126.3 jit_solution(1308733384537942880)
XLA Ops:
  0.0 125.7 %shard_map.28 = f32[128,128]{1,0:T(8,128)S(1)} custom-call(bf16[1,512,512]{2,1,0:T(8,128)(2,1)} %a_hbm.1, bf16[1,64,4096]{2,1,0:T(8,128)(2,1)} %bitcast.1), custom_call_target="tpu_custom_call" | custom-call | tf_op jit(solution)/shard_map/pallas_call | solution.py:478
  125.7 0.6 copy.4

commit v6 on v5

--- a/solution.py
+++ b/solution.py
@@ -26,7 +26,7 @@
 
 def kernel(
     a_hbm, w_hbm, out_ref,
-    abuf, wbuf, yacc, yown, ycat, thl, ubuf, cbuf, rbuf, img, res, dir1, vacc, tok, dots, curv, mblk, obuf,
+    abuf, wbuf, yacc, yown, ycat, thl, ubuf, cbuf, rbuf, img, res, dir1, vacc, tok, dots, curv, mblk, obuf, narrow_parts, narrow_theirs, narrow_whole,
     in_sem, zs, zr, xs, xr, fs, fr, es, er, ys, yr, cs, cr, us, ur, gs, gr, hs, hr, ks, kr, os, orr,
 ):
     mp = lax.axis_index("mp")
@@ -230,41 +230,47 @@
     sibling = dev(x, y, z, 1 - k)
 
     def all_reduce(rnd, block, arrive):
+        narrow = rnd == 2
+        cuts = 1 if narrow else CUTS
+        parts = narrow_parts if narrow else ubuf
+        theirs = narrow_theirs if narrow else rbuf.at[rnd]
+        whole = narrow_whole if narrow else img.at[rnd]
+
         def core_part(o):
             q = at_y(o)
             return remote(ubuf.at[2 * q + 1 - k], cbuf.at[rnd, q], cs.at[rnd, q], cr.at[rnd, q], sibling)
 
         def cut(c):
-            return pl.ds(c * (COLS // CUTS), COLS // CUTS)
+            return pl.ds(c * (COLS // cuts), COLS // cuts)
 
         def ring_part(o, c):
             q = at_y(o)
-            src, dst = ubuf.at[2 * q + k, cut(c)], rbuf.at[rnd, y, cut(c)]
+            src, dst = parts.at[2 * q + k, cut(c)], theirs.at[y, cut(c)]
             return remote(src, dst, us.at[rnd, q, c], ur.at[rnd, y, c], dev(x, q, z, k))
 
         def ring_part_from(o, c):
             q = at_y(o)
-            src, dst = ubuf.at[2 * q + k, cut(c)], rbuf.at[rnd, q, cut(c)]
+            src, dst = parts.at[2 * q + k, cut(c)], theirs.at[q, cut(c)]
             return remote(src, dst, us.at[rnd, q, c], ur.at[rnd, q, c], dev(x, q, z, k))
 
         def ring_whole(o, c):
             q = at_y(o)
-            ref = img.at[rnd, me, cut(c)]
+            ref = whole.at[me, cut(c)]
             return remote(ref, ref, gs.at[rnd, q, c], gr.at[rnd, y, c], dev(x, q, z, k))
 
         def ring_whole_from(o, c):
             q = at_y(o)
-            ref = img.at[rnd, 2 * q + k, cut(c)]
+            ref = whole.at[2 * q + k, cut(c)]
             return remote(ref, ref, gs.at[rnd, q, c], gr.at[rnd, q, c], dev(x, q, z, k))
 
         def core_whole(o):
             q = at_y(o)
-            ref = img.at[rnd, 2 * q + k]
+            ref = whole.at[2 * q + k]
             return remote(ref, ref, hs.at[rnd, q], hr.at[rnd, q], sibling)
 
         def core_whole_from(o):
             q = at_y(o)
-            ref = img.at[rnd, 2 * q + 1 - k]
+            ref = whole.at[2 * q + 1 - k]
             return remote(ref, ref, hs.at[rnd, q], hr.at[rnd, q], sibling)
 
         def give(o):
@@ -278,10 +284,15 @@
             mine = block(b)
             remote(ubuf.at[b], cbuf.at[rnd, q], cs.at[rnd, q], cr.at[rnd, q], sibling).wait_recv()
             if o:
-                ubuf[b] = mine + cbuf[rnd, q]
+                parts[b] = (mine + cbuf[rnd, q]).astype(parts.dtype)
                 ring_part(o, 0).start()
             else:
                 img[rnd, me] = mine + cbuf[rnd, q]
+
+        def widened(b):
+            if narrow:
+                img[rnd, b] = whole[b].astype(F32)
+            arrive(b)
 
         give(2)
         give(1)
@@ -290,35 +301,38 @@
         keep(1)
         give(0)
         keep(3)
-        for c in range(1, CUTS):
+        for c in range(1, cuts):
             for o in (2, 1, 3):
                 ring_part(o, c).start()
         keep(0)
-        for c in range(CUTS):
+        for c in range(cuts):
             for o in (1, 3, 2):
                 ring_part_from(o, c).wait_recv()
-            img[rnd, me, cut(c)] += (
-                rbuf[rnd, at_y(1), cut(c)] + rbuf[rnd, at_y(3), cut(c)] + rbuf[rnd, at_y(2), cut(c)]
+            total = img[rnd, me, cut(c)] + (
+                theirs[at_y(1), cut(c)].astype(F32)
+                + theirs[at_y(3), cut(c)].astype(F32)
+                + theirs[at_y(2), cut(c)].astype(F32)
             )
+            whole[me, cut(c)] = total.astype(whole.dtype)
             for o in (2, 1, 3):
                 ring_whole(o, c).start()
         core_whole(0).start()
-        arrive(me)
+        widened(me)
         core_whole_from(0).wait_recv()
-        arrive(2 * y + 1 - k)
+        widened(2 * y + 1 - k)
         for o in (1, 3, 2):
-            for c in range(CUTS):
+            for c in range(cuts):
                 ring_whole_from(o, c).wait_recv()
             core_whole(o).start()
-            arrive(2 * at_y(o) + k)
+            widened(2 * at_y(o) + k)
         for o in (1, 3, 2):
             core_whole_from(o).wait_recv()
-            arrive(2 * at_y(o) + 1 - k)
+            widened(2 * at_y(o) + 1 - k)
         for o in range(4):
             core_part(o).wait_send()
             core_whole(o).wait_send()
             if o:
-                for c in range(CUTS):
+                for c in range(cuts):
                     ring_part(o, c).wait_send()
                     ring_whole(o, c).wait_send()
 
@@ -499,6 +513,9 @@
             vmem((8, 1, 128), F32),
             vmem((4, COLS, 128), F32),
             vmem((4, COLS, 128), F32),
+            vmem((8, COLS, 512), BF16),
+            vmem((4, COLS, 512), BF16),
+            vmem((8, COLS, 512), BF16),
             dma((2,)),
             dma((2, NP + 1, 8)),
             dma((2, NP + 1, 8)),

time: 126 us -> 125 us (level)
  Pallas kernels: 126 us -> 124 us
    pallas_call x1, Pallas kernels: 126 us -> 124 us  [local(): pl.pallas_call(kernel, out_shape=jax.ShapeDtypeStruct((128, 128), F32), i...]
where the time goes in v6:
time: 125 us; the launch traced here: 124 us
  Pallas kernels  124 us (99%)
    pallas_call x1, Pallas kernels, local(): pl.pallas_call(kernel, out_shape=jax.ShapeDtypeStruct((128, 128), F32), i...  124 us

profile of v6, /device:TPU:17, one launch (start us, length us, event | category | flops | bytes accessed | tf_op | source)
XLA Modules:
  0.0 124.5 jit_solution(652433888141212391)
XLA Ops:
  0.0 123.8 %shard_map.28 = f32[128,128]{1,0:T(8,128)S(1)} custom-call(bf16[1,512,512]{2,1,0:T(8,128)(2,1)} %a_hbm.1, bf16[1,64,4096]{2,1,0:T(8,128)(2,1)} %bitcast.1), custom_call_target="tpu_custom_call" | custom-call | tf_op jit(solution)/shard_map/pallas_call | solution.py:492
  123.8 0.6 copy.4

commit v7 on v6

--- a/solution.py
+++ b/solution.py
@@ -207,38 +207,43 @@
     zrecv(1, NP, 7).wait_recv()
     for i in range(3):
         finish(i, at_z(8)).wait_recv()
-        finish(i, at_z(-7 if i == 0 else 7)).wait_send()
-
-    @pl.loop(1, 8)
-    def _(j):
+
+    def gather_sent():
+        for i in range(3):
+            finish(i, at_z(-7 if i == 0 else 7)).wait_send()
+        for i in range(2):
+            ycopy(i).wait_send()
+
+        @pl.loop(1, 8)
+        def _(j):
+            for d in range(2):
+                for b in (at_z(j), at_z(-j)):
+                    xcopy(d, b).wait_send()
+                    fcopy(d, b).wait_send()
+
         for d in range(2):
-            for b in (at_z(j), at_z(-j)):
-                xcopy(d, b).wait_send()
-                fcopy(d, b).wait_send()
-
-    for d in range(2):
-        for part in range(NP + 1):
-
-            @pl.loop(0, steps(d, part))
-            def _(s):
-                zcopy(d, part, s).wait_send()
+            for part in range(NP + 1):
+
+                @pl.loop(0, steps(d, part))
+                def _(s):
+                    zcopy(d, part, s).wait_send()
 
     for i in range(2):
         yrecv(i).wait_recv()
-        ycopy(i).wait_send()
 
     sibling = dev(x, y, z, 1 - k)
 
-    def all_reduce(rnd, block, arrive):
+    def all_reduce(rnd, block, arrive, meanwhile=None):
         narrow = rnd == 2
         cuts = 1 if narrow else CUTS
-        parts = narrow_parts if narrow else ubuf
+        mine = ubuf.at[rnd]
+        parts = narrow_parts if narrow else mine
         theirs = narrow_theirs if narrow else rbuf.at[rnd]
         whole = narrow_whole if narrow else img.at[rnd]
 
         def core_part(o):
             q = at_y(o)
-            return remote(ubuf.at[2 * q + 1 - k], cbuf.at[rnd, q], cs.at[rnd, q], cr.at[rnd, q], sibling)
+            return remote(mine.at[2 * q + 1 - k], cbuf.at[rnd, q], cs.at[rnd, q], cr.at[rnd, q], sibling)
 
         def cut(c):
             return pl.ds(c * (COLS // cuts), COLS // cuts)
@@ -275,19 +280,19 @@
 
         def give(o):
             b = 2 * at_y(o) + 1 - k
-            ubuf[b] = block(b)
+            mine[b] = block(b)
             core_part(o).start()
 
         def keep(o):
             q = at_y(o)
             b = 2 * q + k
-            mine = block(b)
-            remote(ubuf.at[b], cbuf.at[rnd, q], cs.at[rnd, q], cr.at[rnd, q], sibling).wait_recv()
+            own = block(b)
+            remote(mine.at[b], cbuf.at[rnd, q], cs.at[rnd, q], cr.at[rnd, q], sibling).wait_recv()
             if o:
-                parts[b] = (mine + cbuf[rnd, q]).astype(parts.dtype)
+                parts[b] = (own + cbuf[rnd, q]).astype(parts.dtype)
                 ring_part(o, 0).start()
             else:
-                img[rnd, me] = mine + cbuf[rnd, q]
+                img[rnd, me] = own + cbuf[rnd, q]
 
         def widened(b):
             if narrow:
@@ -305,6 +310,8 @@
             for o in (2, 1, 3):
                 ring_part(o, c).start()
         keep(0)
+        if meanwhile:
+            meanwhile()
         for c in range(cuts):
             for o in (1, 3, 2):
                 ring_part_from(o, c).wait_recv()
@@ -328,13 +335,17 @@
         for o in (1, 3, 2):
             core_whole_from(o).wait_recv()
             widened(2 * at_y(o) + 1 - k)
-        for o in range(4):
-            core_part(o).wait_send()
-            core_whole(o).wait_send()
-            if o:
-                for c in range(cuts):
-                    ring_part(o, c).wait_send()
-                    ring_whole(o, c).wait_send()
+
+        def sent():
+            for o in range(4):
+                core_part(o).wait_send()
+                core_whole(o).wait_send()
+                if o:
+                    for c in range(cuts):
+                        ring_part(o, c).wait_send()
+                        ring_whole(o, c).wait_send()
+
+        return sent
 
     def split(v):
         hi = v.astype(BF16)
@@ -383,7 +394,7 @@
         return go
 
     vacc[...] = jnp.zeros_like(vacc)
-    all_reduce(0, rhs_block, arrived(0, lambda b: img[0, b]))
+    sent0 = all_reduce(0, rhs_block, arrived(0, lambda b: img[0, b]))
     norm = total_of(dots[...])
     for h in range(2):
         t = products(h)
@@ -391,22 +402,25 @@
         tok[0, h] = t
         tok[1, h] = t
     vacc[...] = jnp.zeros_like(vacc)
-    all_reduce(1, image_block, arrived(1, lambda b: img[0, b]))
+    sent1 = all_reduce(1, image_block, arrived(1, lambda b: img[0, b]))
     alpha0 = norm / total_of(dots[...])
     for b in range(8):
         res[b] = img[0, b] - alpha0 * img[1, b]
     norm1 = column_sum(lambda b: res[b] * res[b])
-    beta = norm1 / norm
+    beta0 = norm1 / norm
     for h in range(2):
         t = tok[1, h] - alpha0 * products(h)
         tok[1, h] = t
-        t = t + beta * tok[0, h]
+        t = t + beta0 * tok[0, h]
         tok[0, h] = t
         set_tokens(h, t)
-    for b in range(8):
-        dir1[b] = res[b] + beta * img[0, b]
+
+    def step_direction():
+        for b in range(8):
+            dir1[b] = res[b] + beta0 * img[0, b]
+
     vacc[...] = jnp.zeros_like(vacc)
-    all_reduce(2, image_block, arrived(2, lambda b: dir1[b]))
+    sent2 = all_reduce(2, image_block, arrived(2, lambda b: dir1[b]), step_direction)
     alpha1 = norm1 / total_of(dots[...])
     for b in range(8):
         res[b] = res[b] - alpha1 * img[2, b]
@@ -434,9 +448,7 @@
 
     @pl.loop(1, 8)
     def _(j):
-        b = lax.rem(me + j, 8)
-        krecv(b).wait_recv()
-        kcopy(b).wait_send()
+        krecv(lax.rem(me + j, 8)).wait_recv()
 
     curvature = curv[0]
     for b in range(1, 8):
@@ -465,6 +477,14 @@
         @pl.when(out_self(dx))
         def _():
             obuf[slot] = mblk[dx]
+
+    gather_sent()
+    for sent in (sent0, sent1, sent2):
+        sent()
+
+    @pl.loop(1, 8)
+    def _(j):
+        kcopy(lax.rem(me + j, 8)).wait_send()
 
     for i in range(2):
         for h in range(2):
@@ -501,7 +521,7 @@
             vmem((2 * COLS, 512), BF16),
             vmem((2, COLS, 512), BF16),
             vmem((2, 2 * COLS, 512), BF16),
-            vmem((8, COLS, 512), F32),
+            vmem((3, 8, COLS, 512), F32),
             vmem((3, 4, COLS, 512), F32),
             vmem((3, 4, COLS, 512), F32),
             vmem((3, 8, COLS, 512), F32),

time: 125 us -> 124 us (level)
  no operation moved by 1% of the time
where the time goes in v7:
time: 124 us
  Pallas kernels  123 us (99%)
    pallas_call x1, Pallas kernels, local(): pl.pallas_call(kernel, out_shape=jax.ShapeDtypeStruct((128, 128), F32), i...  123 us

profile of v7, /device:TPU:17, one launch (start us, length us, event | category | flops | bytes accessed | tf_op | source)
XLA Modules:
  0.0 123.9 jit_solution(2564217830693300168)
XLA Ops:
  0.0 123.2 %shard_map.28 = f32[128,128]{1,0:T(8,128)S(1)} custom-call(bf16[1,512,512]{2,1,0:T(8,128)(2,1)} %a_hbm.1, bf16[1,64,4096]{2,1,0:T(8,128)(2,1)} %bitcast.1), custom_call_target="tpu_custom_call" | custom-call | tf_op jit(solution)/shard_map/pallas_call | solution.py:512
  123.2 0.6 copy.4

commit v8 on v7

--- a/solution.py
+++ b/solution.py
@@ -443,8 +443,14 @@
     def _(j):
         kcopy(lax.rem(me + j, 8)).start()
 
-    known = alpha0 * img[0, me] + alpha1 * dir1[me]
-    last = res[me] + beta * dir1[me]
+    def sent_block(dx):
+        return lax.rem(me + 2 * dx, 8)
+
+    known, last = [], []
+    for dx in range(4):
+        b, lanes = sent_block(dx), pl.ds(128 * dx, 128)
+        known.append(alpha0 * img[0, b, :, lanes] + alpha1 * dir1[b, :, lanes])
+        last.append(res[b, :, lanes] + beta * dir1[b, :, lanes])
 
     @pl.loop(1, 8)
     def _(j):
@@ -454,21 +460,24 @@
     for b in range(1, 8):
         curvature = curvature + curv[b]
     alpha2 = norm2 / total_of(jnp.where(diagonal, curvature, 0.0))
-    merged = known + alpha2 * last
 
     origin = lax.rem(zl + 4, 8)
-    to_y, to_z, to_k = lax.div(origin, 2), 8 * lax.rem(origin, 2) + me, lax.div(x, 2)
-    from_y, from_k = lax.div(zl, 2), lax.rem(zl, 2)
+    to_y, to_k = lax.div(origin, 2), lax.div(x, 2)
+    sender = lax.rem(zl + 8 - 2 * x, 8)
+    from_y, from_k = lax.div(sender, 2), lax.rem(sender, 2)
     slot = 2 * lax.rem(x, 2) + zh
 
+    def to_z(dx):
+        return 8 * lax.rem(origin, 2) + sent_block(dx)
+
     def out_self(dx):
-        return (dx == x) & (to_y == y) & (to_z == z) & (to_k == k)
+        return (dx == x) & (to_y == y) & (to_z(dx) == z) & (to_k == k)
 
     def ocopy(dx):
-        return remote(mblk.at[dx], obuf.at[slot], os.at[dx], orr.at[slot], dev(dx, to_y, to_z, to_k))
+        return remote(mblk.at[dx], obuf.at[slot], os.at[dx], orr.at[slot], dev(dx, to_y, to_z(dx), to_k))
 
     for dx in range(4):
-        mblk[dx] = merged[:, 128 * dx : 128 * (dx + 1)]
+        mblk[dx] = known[dx] + alpha2 * last[dx]
 
         @pl.when(jnp.logical_not(out_self(dx)))
         def _():

time: 124 us -> 124 us (level)
  no operation moved by 1% of the time
where the time goes in v8:
time: 124 us
  Pallas kernels  123 us (99%)
    pallas_call x1, Pallas kernels, local(): pl.pallas_call(kernel, out_shape=jax.ShapeDtypeStruct((128, 128), F32), i...  123 us

profile of v8, /device:TPU:17, one launch (start us, length us, event | category | flops | bytes accessed | tf_op | source)
XLA Modules:
  0.0 123.9 jit_solution(3627824340391972439)
XLA Ops:
  0.0 123.3 %shard_map.28 = f32[128,128]{1,0:T(8,128)S(1)} custom-call(bf16[1,512,512]{2,1,0:T(8,128)(2,1)} %a_hbm.1, bf16[1,64,4096]{2,1,0:T(8,128)(2,1)} %bitcast.1), custom_call_target="tpu_custom_call" | custom-call | tf_op jit(solution)/shard_map/pallas_call | solution.py:521
  123.3 0.6 copy.4

commit v9 on v7

--- a/solution.py
+++ b/solution.py
@@ -183,10 +183,8 @@
     finish(1, at_z(7)).start()
     pass_on(at_z(-7))
     finish(0, at_z(-7)).start()
-    for d in (6, -6, 7):
+    for d in (6, -6, 7, -7):
         settle(at_z(d))
-    finish(2, at_z(7)).start()
-    settle(at_z(-7))
 
     yown[...] = yacc[...].astype(BF16)
 
@@ -201,6 +199,7 @@
 
     ycopy(0).start()
     ycopy(1).start()
+    finish(2, at_z(7)).start()
 
     for part in range(NP):
         zrecv(0, part, 7).wait_recv()

time: 124 us -> 123 us (level)
  no operation moved by 1% of the time
where the time goes in v9:
time: 123 us
  Pallas kernels  123 us (100%)
    pallas_call x1, Pallas kernels, local(): pl.pallas_call(kernel, out_shape=jax.ShapeDtypeStruct((128, 128), F32), i...  123 us

profile of v9, /device:TPU:17, one launch (start us, length us, event | category | flops | bytes accessed | tf_op | source)
XLA Modules:
  0.0 123.4 jit_solution(11397274209517637392)
XLA Ops:
  0.0 122.7 %shard_map.28 = f32[128,128]{1,0:T(8,128)S(1)} custom-call(bf16[1,512,512]{2,1,0:T(8,128)(2,1)} %a_hbm.1, bf16[1,64,4096]{2,1,0:T(8,128)(2,1)} %bitcast.1), custom_call_target="tpu_custom_call" | custom-call | tf_op jit(solution)/shard_map/pallas_call | solution.py:511
  122.7 0.6 copy.4

commit v10 on v9

--- a/solution.py
+++ b/solution.py
@@ -8,7 +8,7 @@
 MESH = pl.DeviceIdType.MESH
 F32 = jnp.float32
 BF16 = jnp.bfloat16
-NZ = (96, 80)
+NZ = (80, 80)
 NP = len(NZ)
 ZS = sum(NZ)
 HALF = 176

time: 123 us -> 123 us (level)
  no operation moved by 1% of the time
where the time goes in v10:
time: 123 us
  Pallas kernels  122 us (99%)
    pallas_call x1, Pallas kernels, local(): pl.pallas_call(kernel, out_shape=jax.ShapeDtypeStruct((128, 128), F32), i...  122 us

profile of v10, /device:TPU:17, one launch (start us, length us, event | category | flops | bytes accessed | tf_op | source)
XLA Modules:
  0.0 122.8 jit_solution(15547038214863296406)
XLA Ops:
  0.0 122.1 %shard_map.28 = f32[128,128]{1,0:T(8,128)S(1)} custom-call(bf16[1,512,512]{2,1,0:T(8,128)(2,1)} %a_hbm.1, bf16[1,64,4096]{2,1,0:T(8,128)(2,1)} %bitcast.1), custom_call_target="tpu_custom_call" | custom-call | tf_op jit(solution)/shard_map/pallas_call | solution.py:511
  122.1 0.6 copy.4
